TPU v7x, 512 devices: a whole 4x8x8 slice. The times are simulated.
512 devices in a mesh: panel: 16 (over z_lo, x), tile: 32 (over y, z_hi, core).
Axes of the slice: x: 4, y: 8, z: 8 (z_hi: 2, z_lo: 4; z = z_hi * 4 + z_lo), core: 2. Of those that a mesh axis runs over, the one named last changes fastest.
Arguments:
- snapshots: bfloat16 [128, 256, 2, 512], P('panel', 'tile'), may hold values from -24 to 24
- beam_codes: int32 [32, 256], P(None, 'tile'), may hold values from 0 to 63
- panel_codes: int32 [128], replicated, may hold values from 0 to 63
- loading: float32 [128], P('panel'), may hold values from 1 to 10
Outputs:
- cancel: float32 [128, 62, 2], P('panel')
- beam_out: float32 [2, 512], P(None, 'tile')
All inputs are finite; a program needn't handle non-finite values.
Results may differ from a plain program's by a relative error of at most 0.0036.
Values may be sent and summed in bfloat16 or wider, within the bound.
No kernel may reach another device: no remote copies, remote signals or barrier semaphores. Data moves between devices by JAX's collectives and lax.ppermute only.
A program may use at most 64 MiB of HBM per device.

v0:
```python
import math

import jax
import jax.numpy as jnp
from jax import lax
from jax.sharding import Mesh
from jax.sharding import PartitionSpec as P

SNAPS = 512
TILE = ("tile_0", "tile_1", "tile_2")


phase_levels = 64
array_load = 1.0


def filled_up(lines, length):
    spare = -lines.shape[0] % length
    if not spare:
        return lines
    return jnp.concatenate([lines, jnp.zeros((spare, *lines.shape[1:]), lines.dtype)])


def from_everyone(array, axis):
    length = lax.axis_size(axis)
    return lax.all_to_all(
        jnp.broadcast_to(array[None], (length, *array.shape)), axis, 0, 0, tiled=True
    )


def in_order(tiles, dim):
    tiles = jnp.moveaxis(tiles, 0, dim)
    shape = tiles.shape
    return tiles.reshape(*shape[:dim], shape[dim] * shape[dim + 1], *shape[dim + 2 :])


def gather_axes(array, axes, dim):
    far, near = axes
    first = from_everyone(array, far)
    tiles = jnp.swapaxes(from_everyone(first, near), 0, 1)
    return in_order(tiles.reshape(-1, *array.shape), dim)


def cut_along(array, dim, length):
    shape = array.shape
    tiles = array.reshape(*shape[:dim], length, shape[dim] // length, *shape[dim + 1 :])
    return jnp.moveaxis(tiles, dim, 0)


def summed_on_arrival(array, axis, dim):
    tiles = cut_along(array, dim, lax.axis_size(axis))
    arrived = lax.all_to_all(tiles, axis, split_axis=0, concat_axis=0, tiled=True)
    return arrived.sum(axis=0)


def sum_in_two_steps(array, axes, dim):
    far, near = axes
    tiles = cut_along(array, dim, lax.axis_size(far))
    nearer = summed_on_arrival(tiles, near, dim + 1)
    arrived = lax.all_to_all(nearer, far, split_axis=0, concat_axis=0, tiled=True)
    return arrived.sum(axis=0)


def total_of(array, axes):
    lines = array.reshape(-1, array.shape[-1])
    padded = filled_up(lines, lax.axis_size(axes[0]) * lax.axis_size(axes[1]))
    whole = gather_axes(sum_in_two_steps(padded, axes, 0), axes, 0)
    return lax.slice_in_dim(whole, 0, len(lines)).reshape(array.shape)


def gather_directly(array, axis, dim):
    tiles = from_everyone(array, axis)
    return in_order(tiles, dim)


def over_copies(array, axis):
    everything = from_everyone(array, axis)
    return jnp.sum(everything, axis=0)


def steering_rows(codes, total_tiles):
    angles = codes.astype(jnp.float32) * (2.0 * math.pi / phase_levels)
    cosine = jnp.cos(angles)
    sine = jnp.sin(angles)
    count_beams = codes.shape[0]
    count_tiles = codes.shape[1]
    real_rows = jnp.stack([cosine, sine], axis=-1).reshape(count_beams, 2 * count_tiles)
    imag_rows = jnp.stack([-sine, cosine], axis=-1).reshape(count_beams, 2 * count_tiles)
    table = jnp.stack([real_rows, imag_rows], axis=1).reshape(2 * count_beams, 2 * count_tiles)
    return (table / math.sqrt(total_tiles)).astype(jnp.bfloat16)


def solve_one(factor_one, right_one):
    return jax.scipy.linalg.cho_solve((factor_one, True), right_one)


def cancel_weights(covar):
    factor = jnp.linalg.cholesky(covar[:, 2:, 2:])
    return jax.vmap(solve_one)(factor, covar[:, 2:, :2])


def constraint_matrix(panel_codes):
    angles = panel_codes.astype(jnp.float32) * (2.0 * math.pi / phase_levels)
    cosine = jnp.cos(angles)
    sine = jnp.sin(angles)
    upper = jnp.stack([cosine, -sine], axis=-1)
    lower = jnp.stack([sine, cosine], axis=-1)
    return jnp.stack([upper, lower], axis=1).reshape(2 * panel_codes.shape[0], 2)


def array_weights(covar, constraint):
    factor = jnp.linalg.cholesky(covar)
    solved = jax.scipy.linalg.cho_solve((factor, True), constraint)
    gram = jnp.dot(constraint.T, solved, precision=lax.Precision.HIGHEST)
    determinant = gram[0, 0] * gram[1, 1] - gram[0, 1] * gram[1, 0]
    inverse = (
        jnp.stack([jnp.stack([gram[1, 1], -gram[0, 1]]), jnp.stack([-gram[1, 0], gram[0, 0]])])
        / determinant
    )
    return jnp.dot(solved, inverse, precision=lax.Precision.HIGHEST)


def body(snapshots, beam_codes, panel_codes, loading):
    own_panels = snapshots.shape[0]
    own_tiles = snapshots.shape[1]
    tile_count = lax.axis_size(TILE)
    block_snaps = SNAPS // tile_count
    table = steering_rows(beam_codes, own_tiles * tile_count)
    samples = snapshots.reshape(own_panels, 2 * own_tiles, SNAPS)
    partial_value = jnp.einsum("bk,pks->pbs", table, samples, preferred_element_type=jnp.float32)
    totals = total_of(partial_value, (("tile_0", "tile_1"), "tile_2"))
    summed = jnp.einsum("pis,pjs->pij", totals, totals, precision=lax.Precision.HIGHEST)
    start = lax.axis_index(TILE) * block_snaps
    beams = lax.dynamic_slice_in_dim(totals, start, block_snaps, 2)
    width = beams.shape[1]
    identity = jnp.eye(width, dtype=jnp.float32)
    covar = summed / SNAPS + loading[:, None, None] * identity[None, :, :]
    cancel = cancel_weights(covar)
    outputs = beams[:, :2, :] - jnp.einsum(
        "pak,pas->pks", cancel, beams[:, 2:, :], precision=lax.Precision.HIGHEST
    )
    gathered = gather_directly(outputs, "panel", 0)
    flat = gathered.reshape(gathered.shape[0] * 2, block_snaps)
    own_flat = outputs.reshape(2 * own_panels, block_snaps)
    own_rows = jnp.dot(own_flat, flat.T, precision=lax.Precision.HIGHEST)
    summed_rows = over_copies(own_rows, TILE)
    array_sum = gather_directly(summed_rows, "panel", 0)
    array_covar = array_sum / SNAPS + array_load * jnp.eye(flat.shape[0], dtype=jnp.float32)
    weights = array_weights(array_covar, constraint_matrix(panel_codes))
    beam_out = jnp.dot(weights.T, flat, precision=lax.Precision.HIGHEST) * math.sqrt(
        flat.shape[0] // 2
    )
    return (cancel, beam_out)


def solution(mesh):
    torus = Mesh(
        mesh.devices.reshape(mesh.shape["panel"], 8, 2, 2), ("panel", "tile_0", "tile_1", "tile_2")
    )
    return jax.shard_map(
        body,
        mesh=torus,
        in_specs=(P("panel", TILE, None, None), P(None, TILE), P(), P("panel")),
        out_specs=(P("panel", None, None), P(None, TILE)),
        check_vma=False,
    )
```

profile of v0, /device:TPU:1, one launch (start us, length us, event | category | flops | bytes accessed | tf_op | source)
XLA Modules:
  0.0 287.4 jit_solution(14226904678085471375)
XLA Ops:
  0.6 0.8 fusion.21
  2.0 11.1 %all_to_all.35 = f32[2,16,16,512]{3,2,1,0:T(8,128)S(1)} all-to-all(f32[2,16,16,512]{3,2,1,0:T(8,128)S(1)} %bitcast.109), channel_id=1, replica_groups=mesh['panel'=16,'tile_0'=8,'tile_1'=2,'tile_2'=2] {'tile_2'}, dimensions={0} | all-to-all | bytes 2097152 | tf_op jit(solution)/shard_map/all_to_all | solution.py:52
  13.2 30.8 %all_to_all.36 = f32[16,16,512]{2,1,0:T(8,128)S(1)} all-to-all(f32[16,16,512]{2,1,0:T(8,128)S(1)} %reduce_sum.27), channel_id=1, replica_groups=mesh['panel'=16,'tile_0'=8,'tile_1'=2,'tile_2'=2] {'tile_0','tile_1'}, dimensions={0} | all-to-all | bytes 1048576 | tf_op jit(solution)/shard_map/all_to_all | solution.py:60
  44.0 0.8 broadcast_in_dim.15
  44.9 6.1 %all-to-all-start.2 = ((f32[16,16,512]{2,1,0:T(8,128)}), f32[16,16,512]{2,1,0:T(8,128)S(1)}, u32[]{:S(2)}, u32[]{:S(2)}) async-start(f32[16,16,512]{2,1,0:T(8,128)} %broadcast_in_dim.15), calls=%async_computation.2 | async-start | bytes 1048576 | tf_op jit(solution)/shard_map/all_to_all | solution.py:26
  51.0 20.4 %all-to-all-done.2 = f32[16,16,512]{2,1,0:T(8,128)S(1)} async-done(((f32[16,16,512]{2,1,0:T(8,128)}), f32[16,16,512]{2,1,0:T(8,128)S(1)}, u32[]{:S(2)}, u32[]{:S(2)}) %all-to-all-start.2) | async-done | bytes 524320 | tf_op jit(solution)/shard_map/all_to_all | solution.py:26
  71.6 5.8 %all_to_all.37 = f32[2,16,16,512]{3,2,1,0:T(8,128)S(1)} all-to-all(f32[2,16,16,512]{3,2,1,0:T(8,128)S(1)} %broadcast_in_dim.16), channel_id=1, replica_groups=mesh['panel'=16,'tile_0'=8,'tile_1'=2,'tile_2'=2] {'tile_2'}, dimensions={0} | all-to-all | bytes 2097152 | tf_op jit(solution)/shard_map/all_to_all | solution.py:26
  77.5 0.6 copy-done.3
  78.1 1.1 fusion
  79.7 45.4 %custom-call.29 = f32[8,62,62]{2,1,0:T(8,128)S(1)} custom-call(f32[8,62,62]{2,1,0:T(8,128)S(1)} %fusion.7), custom_call_target="Cholesky" | custom-call | tf_op jit(solution)/shard_map/jit(cholesky)/cholesky | solution.py:98
  125.4 38.1 %custom-call.30 = f32[8,1,62,62]{2,3,1,0:T(8,128)S(1)} custom-call(f32[8,1,62,62]{3,2,1,0:T(8,128)S(1)} %select_bitcast_fusion), custom_call_target="InvertDiagBlocksLowerTriangular" | custom-call | tf_op jit(solution)/shard_map/vmap(jit(_cho_solve))/triangular_solve | solution.py:94
  165.3 12.3 %all_to_all.38 = f32[16,1,256]{2,1,0:T(1,128)S(1)} all-to-all(f32[16,1,256]{2,1,0:T(1,128)S(1)} %reshape.109), channel_id=1, replica_groups=mesh['panel'=16,'tile_0'=8,'tile_1'=2,'tile_2'=2] {'panel'}, dimensions={0} | all-to-all | bytes 32768 | tf_op jit(solution)/shard_map/all_to_all | solution.py:26
  177.6 0.6 broadcast.224
  178.1 0.7 reduce.18
  179.4 26.5 %all_to_all.39 = f32[32,16,256]{2,1,0:T(8,128)S(1)} all-to-all(f32[32,16,256]{2,1,0:T(8,128)S(1)} %broadcast_in_dim.18), channel_id=1, replica_groups=mesh['panel'=16,'tile_0'=8,'tile_1'=2,'tile_2'=2] {'tile_0','tile_1','ti..., dimensions={0} | all-to-all | bytes 1048576 | tf_op jit(solution)/shard_map/all_to_all | solution.py:26
  205.9 0.7 broadcast_in_dim.19
  206.6 3.8 %all-to-all-start.6 = ((f32[16,16,256]{2,1,0:T(8,128)}), f32[16,16,256]{2,1,0:T(8,128)S(1)}, u32[]{:S(2)}, u32[]{:S(2)}) async-start(f32[16,16,256]{2,1,0:T(8,128)} %broadcast_in_dim.19), calls=%async_computation.6 | async-start | bytes 524288 | tf_op jit(solution)/shard_map/all_to_all | solution.py:26
  211.4 7.6 %all-to-all-done.6 = f32[16,16,256]{2,1,0:T(8,128)S(1)} async-done(((f32[16,16,256]{2,1,0:T(8,128)}), f32[16,16,256]{2,1,0:T(8,128)S(1)}, u32[]{:S(2)}, u32[]{:S(2)}) %all-to-all-start.6) | async-done | bytes 262176 | tf_op jit(solution)/shard_map/all_to_all | solution.py:26
  219.5 11.7 %cholesky.124 = f32[128,128]{1,0:T(8,128)S(1)} custom-call(f32[128,128]{1,0:T(8,128)S(1)} %cholesky.154), custom_call_target="Cholesky" | custom-call | tf_op jit(solution)/shard_map/jit(cholesky)/cholesky | solution.py:112
  231.2 9.8 %custom-call.31 = f32[1,128,128]{1,2,0:T(8,128)S(1)} custom-call(f32[1,128,128]{2,1,0:T(8,128)S(1)} %get-tuple-element.23), custom_call_target="InvertDiagBlocksLowerTriangular" | custom-call | tf_op jit(solution)/shard_map/jit(cholesky)/cholesky | solution.py:112
  241.5 11.7 %cholesky.141 = f32[128,128]{1,0:T(8,128)S(1)} custom-call(f32[128,128]{1,0:T(8,128)S(1)} %convolution_subtract_fusion), custom_call_target="Cholesky" | custom-call | tf_op jit(solution)/shard_map/jit(cholesky)/cholesky | solution.py:112
  253.3 0.7 compare_reduce_fusion.1
  255.4 4.1 %while.1 = (s32[]{:T(128)}, f32[256,256]{1,0:T(8,128)S(1)}, s32[2,2]{1,0:T(2,128)S(1)}, f32[2,128,128]{2,1,0:T(8,128)S(1)}, s32[]{:T(128)}) while((s32[]{:T(128)}, f32[256,256]{1,0:T(8,128)S(1)}, s32[2,2]{1,0:T(2,128)S(1)}, f32[2,128,128]{2,1,0:T(8,128)S(1)}, s32[]{:T(128)}) %tuple.37), condition=%wide.while_cond, body=%wide.while_body.sunk | while | flops 2 | bytes 131181 | solution.py:113
  255.4 0.7 fusion.56
  256.1 1.3 bitcast_dynamic-update-slice_fusion.2
  257.4 0.7 fusion.56
  258.1 1.3 bitcast_dynamic-update-slice_fusion.2
  259.4 19.9 %custom-call.32 = f32[2,128,128]{1,2,0:T(8,128)S(1)} custom-call(f32[2,128,128]{2,1,0:T(8,128)S(1)} %get-tuple-element.9), custom_call_target="InvertDiagBlocksLowerTriangular" | custom-call | tf_op jit(solution)/shard_map/jit(_cho_solve)/triangular_solve | solution.py:113
  280.7 0.6 fusion.33
  285.0 0.7 maximum_bitcast_fusion.2
  285.7 0.8 maximum_bitcast_fusion.3
  286.7 0.8 convolution_multiply_fusion.1
  (72 shorter events, 7.3 us)
Async XLA Ops:
  0.6 0.9 copy-start
  44.9 26.6 %all-to-all-start.2 = ((f32[16,16,512]{2,1,0:T(8,128)}), f32[16,16,512]{2,1,0:T(8,128)S(1)}, u32[]{:S(2)}, u32[]{:S(2)}) async-start(f32[16,16,512]{2,1,0:T(8,128)} %broadcast_in_dim.15), calls=%async_computation.2 | async-start | bytes 1048576 | tf_op jit(solution)/shard_map/all_to_all | solution.py:26
  77.5 0.7 copy-start.3
  164.4 0.6 copy-start.1
  206.6 3.9 %copy-start.2 = (s32[128]{0:T(128)S(1)}, s32[128]{0:T(128)}, u32[]{:S(2)}) copy-start(s32[128]{0:T(128)} %param.6) | copy-start | bytes 1540
  206.6 12.5 %all-to-all-start.6 = ((f32[16,16,256]{2,1,0:T(8,128)}), f32[16,16,256]{2,1,0:T(8,128)S(1)}, u32[]{:S(2)}, u32[]{:S(2)}) async-start(f32[16,16,256]{2,1,0:T(8,128)} %broadcast_in_dim.19), calls=%async_computation.6 | async-start | bytes 524288 | tf_op jit(solution)/shard_map/all_to_all | solution.py:26
where the time goes:
time: 290 us; the launch traced here: 287 us
  other arithmetic  141 us (49%)
  blocking collectives  86.4 us (30%)
  waiting for transfers between devices  28.1 us (10%)
  local copies, waits for them, and re-layouts  10 us (3%)
  starting transfers between devices  9.95 us (3%)
  between operations  6.02 us (2%)
  matrix products  5.61 us (2%)
    another operation x4, other arithmetic, cancel_weights(): factor = jnp.linalg.cholesky(covar[:, 2:, 2:])  45.6 us
    all_to_all x3, blocking collectives, from_everyone(): lax.all_to_all(jnp.broadcast_to(array[None], (length, *array.shape)), axi...  44.6 us
    another operation x3, other arithmetic, solve_one(): return jax.scipy.linalg.cho_solve((factor_one, True), right_one)  38.2 us
    another operation x6, other arithmetic, array_weights(): factor = jnp.linalg.cholesky(covar)  34 us
    all_to_all x1, blocking collectives, sum_in_two_steps(): lax.all_to_all(nearer, far, split_axis=0, concat_axis=0, tiled=True)  30.8 us
    all_to_all x2, waiting for transfers between devices, from_everyone(): lax.all_to_all(jnp.broadcast_to(array[None], (length, *array.shape)), axi...  28.1 us
    another operation x3, other arithmetic, array_weights(): solved = jax.scipy.linalg.cho_solve((factor, True), constraint)  19.9 us
    all_to_all x1, blocking collectives, summed_on_arrival(): lax.all_to_all(tiles, axis, split_axis=0, concat_axis=0, tiled=True)  11.1 us
  transfers between devices with their start and end apart: 2, of which 2 were waited for; matrix products, arithmetic and copies ran while one was open for 0% of the time, Pallas kernels for 0%

commit v1 on v0

v1 whole, which is shorter than its diff:
```python
import math

import jax
import jax.numpy as jnp
from jax import lax
from jax.experimental import pallas as pl
from jax.experimental.pallas import tpu as pltpu
from jax.sharding import Mesh
from jax.sharding import PartitionSpec as P

SNAPS = 512
PHASE_LEVELS = 64
ARRAY_LOAD = 1.0
TILE = ("tile_y", "tile_z", "core")
BLOCK = 64
HIGHEST = lax.Precision.HIGHEST


def vmem():
    return pl.BlockSpec(memory_space=pltpu.VMEM)


def smem():
    return pl.BlockSpec(memory_space=pltpu.SMEM)


def lanes_of(block, lane):
    return jnp.broadcast_to(block[:, lane : lane + 1], (8, 128))


def row_of(block, row):
    return jnp.broadcast_to(block[row : row + 1, :], (8, 128))


def eliminate(rows, first_lane, steps):
    rows = [list(row) for row in rows]
    place = lax.broadcasted_iota(jnp.int32, (8, 128), 0)
    for k in range(0, steps, 2):
        own, s = divmod(k, 8)
        lane = first_lane + k
        upper = [row_of(group, s) for group in rows[own]]
        lower = [row_of(group, s + 1) for group in rows[own]]
        left = [lanes_of(row[0], lane) for row in rows]
        right = [lanes_of(row[0], lane + 1) for row in rows]
        a = row_of(left[own], s)
        b = row_of(right[own], s)
        c = row_of(right[own], s + 1)
        scale = 1.0 / (a * c - b * b)
        a, b, c = a * scale, b * scale, c * scale
        for i, row in enumerate(rows):
            f0 = c * left[i] - b * right[i]
            f1 = a * right[i] - b * left[i]
            for g in range(len(row)):
                value = row[g] - f0 * upper[g] - f1 * lower[g]
                if i == own:
                    value = jnp.where(place == s, c * upper[g] - b * lower[g], value)
                    value = jnp.where(place == s + 1, a * lower[g] - b * upper[g], value)
                row[g] = value
    return rows


def beams_kernel(got_ref, beams_ref, covar_ref):
    got = got_ref[...]
    pieces = got[:, 32:40, :].astype(jnp.float32)
    table = jnp.concatenate([pieces, pltpu.roll(pieces, 64, 2)], axis=1)
    table = table.reshape(512, 128).astype(jnp.bfloat16)
    samples = jnp.concatenate(
        [got[:, 0:16, :].reshape(512, 128), got[:, 16:32, :].reshape(512, 128)], axis=1
    )
    beams = lax.dot_general(
        table, samples, (((0,), (0,)), ((), ())), preferred_element_type=jnp.float32
    )[:64]
    beams_ref[...] = beams
    covar_ref[...] = lax.dot_general(
        beams, beams, (((1,), (1,)), ((), ())), precision=HIGHEST, preferred_element_type=jnp.float32
    )


def cancel_kernel(loading_ref, place_ref, beams_ref, own_ref, other_ref, out_ref):
    load = loading_ref[place_ref[0]]
    covar = (own_ref[...] + other_ref[...]) / SNAPS
    row = lax.broadcasted_iota(jnp.int32, (64, 64), 0)
    column = lax.broadcasted_iota(jnp.int32, (64, 64), 1)
    covar = covar + jnp.where(row == column, load, 0.0)
    covar = jnp.concatenate([covar, jnp.zeros((64, 64), jnp.float32)], axis=1)
    solved = eliminate([[covar[8 * i : 8 * i + 8, :]] for i in range(8)], 0, 62)
    whole = jnp.concatenate([row[0] for row in solved], axis=0)
    whole = jnp.concatenate([whole, jnp.zeros((64, 128), jnp.float32)], axis=0)
    turned = whole.T[62:64, :]
    lane = lax.broadcasted_iota(jnp.int32, (2, 128), 1)
    turned = jnp.where(lane < 62, turned, 0.0)
    beams = beams_ref[...]
    outputs = beams[62:64, :] - jnp.dot(
        turned[:, :64], beams, precision=HIGHEST, preferred_element_type=jnp.float32
    )
    out_ref[0:2, :] = outputs[:, 0:128]
    out_ref[2:4, :] = outputs[:, 128:256]
    lane = lax.broadcasted_iota(jnp.int32, (1, 128), 1)
    out_ref[4:5, :] = jnp.where(lane < 64, turned[0:1, :], pltpu.roll(turned, 64, 1)[1:2, :])


def array_kernel(place_ref, codes_ref, own_ref, other_ref, cancel_ref, out_ref, work_ref):
    y = place_ref[0]
    slot = place_ref[1]
    core = place_ref[2]
    panel = place_ref[3]
    cancel_ref[...] = own_ref[pl.ds(panel * 40 + 4, 8, stride=5), :]

    def block(ref, k, b):
        return ref[pl.ds(2 * b + k, 128, stride=5), :]

    def half(ref):
        return jnp.concatenate(
            [
                jnp.concatenate([block(ref, k, 0), block(ref, k, 1)], axis=1)
                for k in range(2)
            ],
            axis=0,
        )

    def square(flat):
        return lax.dot_general(
            flat, flat, (((1,), (1,)), ((), ())), precision=HIGHEST, preferred_element_type=jnp.float32
        )

    own = half(own_ref)
    other = half(other_ref)
    row = lax.broadcasted_iota(jnp.int32, (256, 256), 0)
    column = lax.broadcasted_iota(jnp.int32, (256, 256), 1)
    covar = (square(own) + square(other)) / SNAPS + jnp.where(row == column, ARRAY_LOAD, 0.0)

    angles = codes_ref[...].astype(jnp.float32) * (2.0 * math.pi / PHASE_LEVELS)
    cosine = jnp.cos(angles)
    sine = jnp.sin(angles)
    spread_cosine = jnp.broadcast_to(cosine, (128, 128)).T
    spread_sine = jnp.broadcast_to(sine, (128, 128)).T

    mine = jnp.where(core == y // 4, own, other)
    mine = jnp.where((y % 4) // 2 == 0, mine[:, :128], mine[:, 128:])
    mine = pltpu.roll(mine, lax.rem(128 - 16 * slot, 128), 1)
    lane = lax.broadcasted_iota(jnp.int32, (128, 128), 1)

    def right_side(values, first, second):
        values = jnp.where(lane < 16, values, 0.0)
        return jnp.where(lane == 16, first, jnp.where(lane == 17, second, values))

    work_ref[0:256, 0:256] = covar
    work_ref[0:128, 256:384] = right_side(mine[:128], spread_cosine, -spread_sine)
    work_ref[128:256, 256:384] = right_side(mine[128:], spread_sine, spread_cosine)
    work_ref[256:264, :] = jnp.zeros((8, 384), jnp.float32)
    work_ref[256:257, 0:128] = cosine
    work_ref[256:257, 128:256] = sine
    work_ref[257:258, 0:128] = -sine
    work_ref[257:258, 128:256] = cosine

    for start in range(0, 256, BLOCK):
        stop = start + BLOCK
        first = start // 128
        groups = list(range(first, 3))
        rows = [
            [work_ref[r : r + 8, 128 * g : 128 * g + 128] for g in groups]
            for r in range(start, stop, 8)
        ]
        rows = eliminate(rows, start % 128, BLOCK)
        if stop % 128 == 0:
            groups, rows = groups[1:], [row[1:] for row in rows]
        solved = jnp.concatenate([jnp.concatenate(row, axis=1) for row in rows], axis=0)
        lines = [solved]
        width = solved.shape[1]
        before, after = start % 128, 128 - start % 128 - BLOCK
        if before:
            lines = [jnp.zeros((before, width), jnp.float32)] + lines
        if after:
            lines = lines + [jnp.zeros((after, width), jnp.float32)]
        solved = jnp.concatenate(lines, axis=0) if len(lines) > 1 else solved
        cuts = [(stop, stop + BLOCK), (stop + BLOCK, 264)] if stop < 256 else [(256, 264)]
        left = 128 * groups[0]
        for top, bottom in cuts:
            if top >= bottom:
                continue
            factor = work_ref[top:bottom, 128 * first : 128 * first + 128]
            work_ref[top:bottom, left:384] = work_ref[top:bottom, left:384] - jnp.dot(
                factor, solved, precision=HIGHEST, preferred_element_type=jnp.float32
            )

    final = -work_ref[256:264, 256:384]
    upper = row_of(final, 0)
    lower = row_of(final, 1)
    g00 = lanes_of(upper, 16)
    g01 = lanes_of(upper, 17)
    g10 = lanes_of(lower, 16)
    g11 = lanes_of(lower, 17)
    scale = math.sqrt(128.0) / (g00 * g11 - g01 * g10)
    first_row = (g11 * upper - g10 * lower) * scale
    second_row = (g00 * lower - g01 * upper) * scale
    place = lax.broadcasted_iota(jnp.int32, (8, 128), 0)
    out_ref[...] = jnp.where(place == 0, first_row, second_row)[0:2, 0:16]


def steering_columns(codes):
    angles = codes.T.astype(jnp.float32) * (2.0 * math.pi / PHASE_LEVELS)
    cosine = jnp.cos(angles)
    sine = jnp.sin(angles)
    real = jnp.stack([cosine, -sine], axis=-1)
    imag = jnp.stack([sine, cosine], axis=-1)
    tiles, beams = angles.shape
    table = jnp.stack([real, imag], axis=1).reshape(2 * tiles, 2 * beams)
    table = (table / math.sqrt(256)).astype(jnp.bfloat16)
    return jnp.concatenate([table[:, 2:], table[:, :2]], axis=1)


def body(snapshots, beam_codes, panel_codes, loading):
    y = lax.axis_index("tile_y")
    z = lax.axis_index("tile_z")
    core = lax.axis_index("core")
    panel = lax.axis_index("panel")
    table = steering_columns(beam_codes)
    table = jnp.concatenate([table[:8], table[8:]], axis=1)
    samples = snapshots.reshape(8, 16, 2, 2, 128)
    samples = samples.transpose(0, 2, 3, 1, 4).reshape(8, 2, 32, 128)
    table = jnp.broadcast_to(table[None, None], (8, 2, 8, 128))
    message = jnp.concatenate([samples, table], axis=2)
    message = jnp.broadcast_to(message[:, None], (8, 2, 2, 40, 128)).reshape(32, 40, 128)
    got = lax.all_to_all(message, TILE, 0, 0, tiled=True)
    beams, covar = pl.pallas_call(
        beams_kernel,
        out_shape=(
            jax.ShapeDtypeStruct((64, 256), jnp.float32),
            jax.ShapeDtypeStruct((64, 64), jnp.float32),
        ),
        in_specs=[vmem()],
        out_specs=(vmem(), vmem()),
        name="beams",
    )(got)
    other = lax.ppermute(covar, "core", [(0, 1), (1, 0)])
    line = pl.pallas_call(
        cancel_kernel,
        out_shape=jax.ShapeDtypeStruct((5, 128), jnp.float32),
        in_specs=[smem(), smem(), vmem(), vmem(), vmem()],
        out_specs=vmem(),
        name="cancel",
    )(loading, y.reshape(1), beams, covar, other)
    lines = jnp.broadcast_to(line.reshape(1, 5, 1, 128), (128, 5, 1, 128))
    gathered = lax.all_to_all(lines, ("panel", "tile_y"), 0, 0, tiled=True)
    gathered = gathered.reshape(640, 128)
    other = lax.ppermute(gathered, "core", [(0, 1), (1, 0)])
    slot = (y % 2) * 4 + z * 2 + core
    place = jnp.stack([y, slot, core, panel]).astype(jnp.int32)
    cancel, beam_out = pl.pallas_call(
        array_kernel,
        out_shape=(
            jax.ShapeDtypeStruct((8, 128), jnp.float32),
            jax.ShapeDtypeStruct((2, 16), jnp.float32),
        ),
        in_specs=[smem(), vmem(), vmem(), vmem()],
        out_specs=(vmem(), vmem()),
        scratch_shapes=[pltpu.VMEM((264, 384), jnp.float32)],
        name="array",
    )(place, panel_codes.reshape(1, 128), gathered, other)
    cancel = cancel.reshape(8, 2, 64)[:, :, :62].transpose(0, 2, 1)
    return cancel, beam_out


def solution(mesh):
    torus = Mesh(
        mesh.devices.reshape(mesh.shape["panel"], 8, 2, 2), ("panel", "tile_y", "tile_z", "core")
    )
    return jax.shard_map(
        body,
        mesh=torus,
        in_specs=(P("panel", TILE, None, None), P(None, TILE), P(), P("panel")),
        out_specs=(P("panel", None, None), P(None, TILE)),
        check_vma=False,
    )
```

time: 290 us -> 105 us (0.36)
  other arithmetic: 141 us -> 1.68 us
  Pallas kernels: 0 us -> 29.9 us
  blocking collectives: 86.4 us -> 59.2 us
  waiting for transfers between devices: 28.1 us -> 1.43 us
  matrix products: 5.61 us -> 0 us
  local copies, waits for them, and re-layouts: 10 us -> 4.47 us
  between operations: 6.02 us -> 0.75 us
    another operation x24 -> x4, other arithmetic: 140 us -> 1.5 us  [the longest x1 0.79 us: steering_columns(): real = jnp.stack([cosine, -sine], axis=-1)]
    pallas_call x0 -> x3, Pallas kernels: none -> 29.9 us  [the longest x1 21.8 us: body(): pl.pallas_call(array_kernel, out_shape=(jax.ShapeDtypeStruct((8, 128), jn...]
    all_to_all x2 -> x0, waiting for transfers between devices: 28.1 us -> none  [from_everyone(): lax.all_to_all(jnp.broadcast_to(array[None], (length, *array.shape)), axi...]
    all_to_all x5 -> x2, blocking collectives: 86.4 us -> 59.2 us  [the longest x1 32.8 us: body(): got = lax.all_to_all(message, TILE, 0, 0, tiled=True)]
    all_to_all x2 -> x0, starting transfers between devices: 9.95 us -> none  [from_everyone(): lax.all_to_all(jnp.broadcast_to(array[None], (length, *array.shape)), axi...]
    ppermute x0 -> x2, starting transfers between devices: none -> 7.22 us  [the longest x1 3.91 us: body(): other = lax.ppermute(gathered, 'core', [(0, 1), (1, 0)])]
    another operation x17 -> x0, local copies, waits for them, and re-layouts: 4.86 us -> none
    dot_general x7 -> x0, matrix products: 3.09 us -> none  [the longest x1 1.08 us: body(): jnp.einsum('pis,pjs->pij', totals, totals, precision=lax.Precision.HIGHEST)]
  transfers between devices with their start and end apart: 2 -> 2, of which waited for: 2 -> 2; matrix products, arithmetic and copies ran while one was open for 0% -> 1% of each run, Pallas kernels for 0% -> 0%
where the time goes in v1:
time: 105 us
  blocking collectives  59.2 us (56%)
  Pallas kernels  29.9 us (28%)
  starting transfers between devices  7.22 us (7%)
  local copies, waits for them, and re-layouts  4.47 us (4%)
  other arithmetic  1.68 us (2%)
  waiting for transfers between devices  1.43 us (1%)
    all_to_all x1, blocking collectives, body(): got = lax.all_to_all(message, TILE, 0, 0, tiled=True)  32.8 us
    all_to_all x1, blocking collectives, body(): gathered = lax.all_to_all(lines, ('panel', 'tile_y'), 0, 0, tiled=True)  26.4 us
    pallas_call x1, Pallas kernels, body(): pl.pallas_call(array_kernel, out_shape=(jax.ShapeDtypeStruct((8, 128), jn...  21.8 us
    pallas_call x1, Pallas kernels, body(): pl.pallas_call(cancel_kernel, out_shape=jax.ShapeDtypeStruct((5, 128), jn...  6 us
    ppermute x1, starting transfers between devices, body(): other = lax.ppermute(gathered, 'core', [(0, 1), (1, 0)])  3.91 us
    ppermute x1, starting transfers between devices, body(): other = lax.ppermute(covar, 'core', [(0, 1), (1, 0)])  3.31 us
    pallas_call x1, Pallas kernels, body(): pl.pallas_call(beams_kernel, out_shape=(jax.ShapeDtypeStruct((64, 256), j...  2.1 us
  transfers between devices with their start and end apart: 2, of which 2 were waited for; matrix products, arithmetic and copies ran while one was open for 1% of the time, Pallas kernels for 0%

profile of v1, /device:TPU:1, one launch (start us, length us, event | category | flops | bytes accessed | tf_op | source)
XLA Modules:
  0.0 104.6 jit_solution(16596961008723882088)
XLA Ops:
  0.6 0.0 copy-start.4
  0.6 0.8 fusion.1
  1.4 0.0 copy-done.4
  1.5 0.0 copy-start.2
  1.5 0.2 copy.12
  1.7 0.2 convert_element_type.12
  1.9 0.1 slice.20
  2.0 0.1 fusion.4
  2.1 0.1 fusion.5
  2.2 0.3 copy-done.2
  2.4 0.1 reshape.39
  2.6 32.8 %all_to_all.10.got_ref = bf16[32,40,128]{2,1,0:T(8,128)(2,1)} all-to-all(bf16[32,40,128]{2,1,0:T(8,128)(2,1)S(1)} %bitcast.34), channel_id=1, replica_groups=mesh['panel'=16,'tile_y'=8,'tile_z'=2,'core'=2] {'tile_y','tile_z','core'}, dimensions={0} | all-to-all | bytes 655360 | tf_op jit(solution)/shard_map/all_to_all | solution.py:224
  35.4 2.1 %beams.1 = (f32[64,256]{1,0:T(8,128)}, f32[64,64]{1,0:T(8,128)}) custom-call(bf16[32,40,128]{2,1,0:T(8,128)(2,1)} %all_to_all.10.got_ref), custom_call_target="tpu_custom_call" | custom-call | tf_op jit(solution)/shard_map/beams/pallas_call | solution.py:225
  37.5 3.3 %collective-permute-start = (f32[64,64]{1,0:T(8,128)}, f32[64,64]{1,0:T(8,128)S(1)}, u32[]{:S(2)}, u32[]{:S(2)}) collective-permute-start(f32[64,64]{1,0:T(8,128)} %get-tuple-element.7.own_ref), channel_id=1, source_target_pairs={{0,1},{1,0},{2,3},{3,2},{4,5},{5,4},{6,7},{7,6},{8,9},{9,8},{10,11... | collective-permute-start | bytes 49160 | tf_op jit(solution)/shard_map/ppermute | solution.py:235
  40.9 1.0 collective-permute-done.other_ref
  41.9 0.0 copy-start.3
  41.9 0.6 copy-done.3
  42.5 6.0 %cancel.1 = f32[5,128]{1,0:T(8,128)} custom-call(f32[8]{0:T(128)} %loading_ref.1, s32[1]{0:T(128)} %bitcast.place_ref, f32[64,256]{1,0:T(8,128)} %get-tuple-element.6.beams_ref, f32[64,64]{1,0:T(8,128)} %get-tuple-element.7.own_ref, f32[64,64]{1,0:T(8,128)} %copy-done.3), custom_call_target="tpu_custom_call" | custom-call | tf_op jit(solution)/shard_map/cancel/pallas_call | solution.py:236
  48.5 0.9 broadcast_in_dim.8
  49.4 26.4 %all_to_all.11 = f32[128,5,1,128]{3,2,1,0:T(1,128)S(1)} all-to-all(f32[128,5,1,128]{3,2,1,0:T(1,128)S(1)} %broadcast_in_dim.8), channel_id=1, replica_groups=mesh['panel'=16,'tile_y'=8,'tile_z'=2,'core'=2] {'panel','tile_y'}, dimensions={0} | all-to-all | bytes 655360 | tf_op jit(solution)/shard_map/all_to_all | solution.py:244
  75.8 0.0 copy-start
  75.8 3.9 %collective-permute-start.1 = (f32[640,128]{1,0:T(8,128)S(1)}, f32[640,128]{1,0:T(8,128)S(1)}, u32[]{:S(2)}, u32[]{:S(2)}) collective-permute-start(f32[640,128]{1,0:T(8,128)S(1)} %bitcast.32), channel_id=1, source_target_pairs={{0,1},{1,0},{2,3},{3,2},{4,5},{5,4},{6,7},{7,6},{8,9},{9,8},{10,11... | collective-permute-start | bytes 983048 | tf_op jit(solution)/shard_map/ppermute | solution.py:246
  79.7 0.7 pad_add_fusion.place_ref
  80.4 0.4 collective-permute-done.1.other_ref
  80.8 0.0 copy-start.1
  80.8 0.0 copy-done
  80.8 0.7 copy-done.1
  81.5 21.8 %array.1 = (f32[8,128]{1,0:T(8,128)}, f32[2,16]{1,0:T(2,128)}) custom-call(s32[4]{0:T(128)} %pad_add_fusion.place_ref, s32[1,128]{1,0:T(1,128)} %bitcast.39, f32[640,128]{1,0:T(8,128)} %bitcast.33, f32[640,128]{1,0:T(8,128)} %copy-done.1), custom_call_target="tpu_custom_call" | custom-call | tf_op jit(solution)/shard_map/array/pallas_call | solution.py:249
  103.3 0.8 reshape.38
  104.0 0.6 slice_bitcast_fusion
  (7 shorter events, 0.1 us)
Async XLA Ops:
  0.6 0.8 copy-start.4
  1.5 0.9 copy-start.2
  37.5 4.4 %collective-permute-start = (f32[64,64]{1,0:T(8,128)}, f32[64,64]{1,0:T(8,128)S(1)}, u32[]{:S(2)}, u32[]{:S(2)}) collective-permute-start(f32[64,64]{1,0:T(8,128)} %get-tuple-element.7.own_ref), channel_id=1, source_target_pairs={{0,1},{1,0},{2,3},{3,2},{4,5},{5,4},{6,7},{7,6},{8,9},{9,8},{10,11... | collective-permute-start | bytes 49160 | tf_op jit(solution)/shard_map/ppermute | solution.py:235
  41.9 0.6 copy-start.3
  75.8 5.0 %copy-start = (f32[128,5,1,128]{3,2,1,0:T(1,128)}, f32[128,5,1,128]{3,2,1,0:T(1,128)S(1)}, u32[]{:S(2)}) copy-start(f32[128,5,1,128]{3,2,1,0:T(1,128)S(1)} %all_to_all.11) | copy-start | bytes 983044
  75.8 5.0 %collective-permute-start.1 = (f32[640,128]{1,0:T(8,128)S(1)}, f32[640,128]{1,0:T(8,128)S(1)}, u32[]{:S(2)}, u32[]{:S(2)}) collective-permute-start(f32[640,128]{1,0:T(8,128)S(1)} %bitcast.32), channel_id=1, source_target_pairs={{0,1},{1,0},{2,3},{3,2},{4,5},{5,4},{6,7},{7,6},{8,9},{9,8},{10,11... | collective-permute-start | bytes 983048 | tf_op jit(solution)/shard_map/ppermute | solution.py:246
  80.8 0.7 copy-start.1

commit v2 on v1

--- a/solution.py
+++ b/solution.py
@@ -12,7 +12,8 @@
 PHASE_LEVELS = 64
 ARRAY_LOAD = 1.0
 TILE = ("tile_y", "tile_z", "core")
-BLOCK = 64
+BLOCK = 32
+CHUNK = 8
 HIGHEST = lax.Precision.HIGHEST
 
 
@@ -22,6 +23,10 @@
 
 def smem():
     return pl.BlockSpec(memory_space=pltpu.SMEM)
+
+
+def limit(mebibytes):
+    return pltpu.CompilerParams(vmem_limit_bytes=mebibytes << 20)
 
 
 def lanes_of(block, lane):
@@ -35,28 +40,79 @@
 def eliminate(rows, first_lane, steps):
     rows = [list(row) for row in rows]
     place = lax.broadcasted_iota(jnp.int32, (8, 128), 0)
-    for k in range(0, steps, 2):
-        own, s = divmod(k, 8)
-        lane = first_lane + k
-        upper = [row_of(group, s) for group in rows[own]]
-        lower = [row_of(group, s + 1) for group in rows[own]]
-        left = [lanes_of(row[0], lane) for row in rows]
-        right = [lanes_of(row[0], lane + 1) for row in rows]
-        a = row_of(left[own], s)
-        b = row_of(right[own], s)
-        c = row_of(right[own], s + 1)
-        scale = 1.0 / (a * c - b * b)
-        a, b, c = a * scale, b * scale, c * scale
-        for i, row in enumerate(rows):
-            f0 = c * left[i] - b * right[i]
-            f1 = a * right[i] - b * left[i]
-            for g in range(len(row)):
-                value = row[g] - f0 * upper[g] - f1 * lower[g]
+    for first in range(0, steps, CHUNK):
+        count = min(CHUNK, steps - first)
+        spread = [[lanes_of(row[0], first_lane + first + u) for u in range(count)] for row in rows]
+        for t in range(count):
+            own, s = divmod(first + t, 8)
+            scale = 1.0 / row_of(spread[own][t], s)
+            lead = {u: row_of(spread[own][u], s) for u in range(t + 1, count)}
+            upper = [row_of(group, s) for group in rows[own]]
+            for i, row in enumerate(rows):
+                f = spread[i][t]
                 if i == own:
-                    value = jnp.where(place == s, c * upper[g] - b * lower[g], value)
-                    value = jnp.where(place == s + 1, a * lower[g] - b * upper[g], value)
-                row[g] = value
+                    for u in lead:
+                        value = spread[i][u] - (f * lead[u]) * scale
+                        spread[i][u] = jnp.where(place == s, lead[u] * scale, value)
+                    for g in range(len(row)):
+                        value = row[g] - (f * upper[g]) * scale
+                        row[g] = jnp.where(place == s, upper[g] * scale, value)
+                else:
+                    f = f * scale
+                    for u in lead:
+                        spread[i][u] = spread[i][u] - f * lead[u]
+                    for g in range(len(row)):
+                        row[g] = row[g] - f * upper[g]
     return rows
+
+
+def cosine_of(steps):
+    quarter = (steps + 8) >> 4
+    angle = (steps - 16 * quarter).astype(jnp.float32) * (2.0 * math.pi / PHASE_LEVELS)
+    square = angle * angle
+    cosine = 1.0 + square * (
+        -1 / 2 + square * (1 / 24 + square * (-1 / 720 + square * (1 / 40320 - square / 3628800)))
+    )
+    sine = angle * (
+        1.0 + square * (-1 / 6 + square * (1 / 120 + square * (-1 / 5040 + square / 362880)))
+    )
+    value = jnp.where((quarter & 1) == 0, cosine, sine)
+    return jnp.where(((quarter + 1) & 2) == 0, value, -value)
+
+
+def message_kernel(samples_ref, codes_ref, out_ref):
+    codes = jnp.concatenate([codes_ref[...], jnp.zeros((8, 96), jnp.int32)], axis=1)
+    row = lax.broadcasted_iota(jnp.int32, (8, 128), 0)
+    lane = lax.broadcasted_iota(jnp.int32, (8, 128), 1)
+    column = lane & 63
+
+    def placed(values, offset):
+        real = pltpu.roll(values, (offset + 127) % 128, 1)
+        imag = pltpu.roll(values, offset + 30, 1)
+        last = pltpu.roll(values, offset + 62, 1)
+        twin = pltpu.roll(values, offset + 63, 1)
+        values = jnp.where(column < 31, real, jnp.where(column < 62, imag, last))
+        return jnp.where(column == 63, twin, values)
+
+    def doubled(values, first):
+        result = row_of(values, first)
+        for t in range(1, 4):
+            result = jnp.where(row >= 2 * t, row_of(values, first + t), result)
+        return result
+
+    spread = jnp.where(lane < 64, doubled(placed(codes, 0), 0), doubled(placed(codes, 64), 4))
+    imaginary = jnp.where((column >= 31) & (column != 62), 1, 0)
+    table = cosine_of(spread + 16 * (imaginary - (row & 1)))
+    table = (table / math.sqrt(256)).astype(jnp.bfloat16)
+    for p in range(8):
+        for c in range(2):
+            for b in range(2):
+                start = 256 * c + 128 * b
+                value = samples_ref[p, :, start : start + 128]
+                for z in range(2):
+                    out_ref[4 * p + 2 * z + c, 16 * b : 16 * b + 16, :] = value
+            for z in range(2):
+                out_ref[4 * p + 2 * z + c, 32:40, :] = table
 
 
 def beams_kernel(got_ref, beams_ref, covar_ref):
@@ -76,8 +132,8 @@
     )
 
 
-def cancel_kernel(loading_ref, place_ref, beams_ref, own_ref, other_ref, out_ref):
-    load = loading_ref[place_ref[0]]
+def cancel_kernel(loading_ref, beams_ref, own_ref, other_ref, out_ref):
+    load = loading_ref[lax.axis_index("tile_y")]
     covar = (own_ref[...] + other_ref[...]) / SNAPS
     row = lax.broadcasted_iota(jnp.int32, (64, 64), 0)
     column = lax.broadcasted_iota(jnp.int32, (64, 64), 1)
@@ -88,23 +144,42 @@
     whole = jnp.concatenate([whole, jnp.zeros((64, 128), jnp.float32)], axis=0)
     turned = whole.T[62:64, :]
     lane = lax.broadcasted_iota(jnp.int32, (2, 128), 1)
-    turned = jnp.where(lane < 62, turned, 0.0)
+    turned = jnp.where(lane < 62, turned, 0.0)[:, :64]
     beams = beams_ref[...]
     outputs = beams[62:64, :] - jnp.dot(
-        turned[:, :64], beams, precision=HIGHEST, preferred_element_type=jnp.float32
-    )
-    out_ref[0:2, :] = outputs[:, 0:128]
-    out_ref[2:4, :] = outputs[:, 128:256]
-    lane = lax.broadcasted_iota(jnp.int32, (1, 128), 1)
-    out_ref[4:5, :] = jnp.where(lane < 64, turned[0:1, :], pltpu.roll(turned, 64, 1)[1:2, :])
-
-
-def array_kernel(place_ref, codes_ref, own_ref, other_ref, cancel_ref, out_ref, work_ref):
-    y = place_ref[0]
-    slot = place_ref[1]
-    core = place_ref[2]
-    panel = place_ref[3]
-    cancel_ref[...] = own_ref[pl.ds(panel * 40 + 4, 8, stride=5), :]
+        turned, beams, precision=HIGHEST, preferred_element_type=jnp.float32
+    )
+    row = lax.broadcasted_iota(jnp.int32, (64, 64), 0)
+    column = lax.broadcasted_iota(jnp.int32, (64, 64), 1)
+    source = jnp.where(column < 62, column // 2 + 31 * (column & 1), column)
+    paired = jnp.dot(
+        turned,
+        jnp.where(row == source, 1.0, 0.0),
+        precision=HIGHEST,
+        preferred_element_type=jnp.float32,
+    )
+    line = jnp.concatenate(
+        [
+            outputs[:, 0:128],
+            outputs[:, 128:256],
+            jnp.concatenate([paired[0:1, :], paired[1:2, :]], axis=1),
+        ],
+        axis=0,
+    )
+    for i in range(8):
+        out_ref[5 * i : 5 * i + 5, :] = line
+    lines = out_ref[0:40, :]
+    for i in range(1, 16):
+        out_ref[40 * i : 40 * i + 40, :] = lines
+
+
+def array_kernel(codes_ref, own_ref, other_ref, cancel_ref, out_ref, work_ref):
+    y = lax.axis_index("tile_y")
+    core = lax.axis_index("core")
+    slot = (y % 2) * 4 + lax.axis_index("tile_z") * 2 + core
+    cancel = own_ref[pl.ds(lax.axis_index("panel") * 40 + 4, 8, stride=5), :]
+    cancel_ref[:, 0, :] = cancel[:, :62]
+    cancel_ref[:, 1, :] = pltpu.roll(cancel, 64, 1)[:, :62]
 
     def block(ref, k, b):
         return ref[pl.ds(2 * b + k, 128, stride=5), :]
@@ -129,9 +204,8 @@
     column = lax.broadcasted_iota(jnp.int32, (256, 256), 1)
     covar = (square(own) + square(other)) / SNAPS + jnp.where(row == column, ARRAY_LOAD, 0.0)
 
-    angles = codes_ref[...].astype(jnp.float32) * (2.0 * math.pi / PHASE_LEVELS)
-    cosine = jnp.cos(angles)
-    sine = jnp.sin(angles)
+    cosine = cosine_of(codes_ref[...])
+    sine = cosine_of(codes_ref[...] - 16)
     spread_cosine = jnp.broadcast_to(cosine, (128, 128)).T
     spread_sine = jnp.broadcast_to(sine, (128, 128)).T
 
@@ -197,30 +271,15 @@
     out_ref[...] = jnp.where(place == 0, first_row, second_row)[0:2, 0:16]
 
 
-def steering_columns(codes):
-    angles = codes.T.astype(jnp.float32) * (2.0 * math.pi / PHASE_LEVELS)
-    cosine = jnp.cos(angles)
-    sine = jnp.sin(angles)
-    real = jnp.stack([cosine, -sine], axis=-1)
-    imag = jnp.stack([sine, cosine], axis=-1)
-    tiles, beams = angles.shape
-    table = jnp.stack([real, imag], axis=1).reshape(2 * tiles, 2 * beams)
-    table = (table / math.sqrt(256)).astype(jnp.bfloat16)
-    return jnp.concatenate([table[:, 2:], table[:, :2]], axis=1)
-
-
 def body(snapshots, beam_codes, panel_codes, loading):
-    y = lax.axis_index("tile_y")
-    z = lax.axis_index("tile_z")
-    core = lax.axis_index("core")
-    panel = lax.axis_index("panel")
-    table = steering_columns(beam_codes)
-    table = jnp.concatenate([table[:8], table[8:]], axis=1)
-    samples = snapshots.reshape(8, 16, 2, 2, 128)
-    samples = samples.transpose(0, 2, 3, 1, 4).reshape(8, 2, 32, 128)
-    table = jnp.broadcast_to(table[None, None], (8, 2, 8, 128))
-    message = jnp.concatenate([samples, table], axis=2)
-    message = jnp.broadcast_to(message[:, None], (8, 2, 2, 40, 128)).reshape(32, 40, 128)
+    message = pl.pallas_call(
+        message_kernel,
+        out_shape=jax.ShapeDtypeStruct((32, 40, 128), jnp.bfloat16),
+        in_specs=[vmem(), vmem()],
+        out_specs=vmem(),
+        compiler_params=limit(4),
+        name="message",
+    )(snapshots.reshape(8, 16, SNAPS), beam_codes.T)
     got = lax.all_to_all(message, TILE, 0, 0, tiled=True)
     beams, covar = pl.pallas_call(
         beams_kernel,
@@ -230,35 +289,35 @@
         ),
         in_specs=[vmem()],
         out_specs=(vmem(), vmem()),
+        compiler_params=limit(4),
         name="beams",
     )(got)
     other = lax.ppermute(covar, "core", [(0, 1), (1, 0)])
-    line = pl.pallas_call(
+    lines = pl.pallas_call(
         cancel_kernel,
-        out_shape=jax.ShapeDtypeStruct((5, 128), jnp.float32),
-        in_specs=[smem(), smem(), vmem(), vmem(), vmem()],
+        out_shape=jax.ShapeDtypeStruct((640, 128), jnp.float32),
+        in_specs=[smem(), vmem(), vmem(), vmem()],
         out_specs=vmem(),
+        compiler_params=limit(4),
         name="cancel",
-    )(loading, y.reshape(1), beams, covar, other)
-    lines = jnp.broadcast_to(line.reshape(1, 5, 1, 128), (128, 5, 1, 128))
+    )(loading, beams, covar, other)
+    lines = lines.reshape(128, 5, 1, 128)
     gathered = lax.all_to_all(lines, ("panel", "tile_y"), 0, 0, tiled=True)
     gathered = gathered.reshape(640, 128)
     other = lax.ppermute(gathered, "core", [(0, 1), (1, 0)])
-    slot = (y % 2) * 4 + z * 2 + core
-    place = jnp.stack([y, slot, core, panel]).astype(jnp.int32)
     cancel, beam_out = pl.pallas_call(
         array_kernel,
         out_shape=(
-            jax.ShapeDtypeStruct((8, 128), jnp.float32),
+            jax.ShapeDtypeStruct((8, 2, 62), jnp.float32),
             jax.ShapeDtypeStruct((2, 16), jnp.float32),
         ),
-        in_specs=[smem(), vmem(), vmem(), vmem()],
+        in_specs=[vmem(), vmem(), vmem()],
         out_specs=(vmem(), vmem()),
         scratch_shapes=[pltpu.VMEM((264, 384), jnp.float32)],
+        compiler_params=limit(8),
         name="array",
-    )(place, panel_codes.reshape(1, 128), gathered, other)
-    cancel = cancel.reshape(8, 2, 64)[:, :, :62].transpose(0, 2, 1)
-    return cancel, beam_out
+    )(panel_codes.reshape(1, 128), gathered, other)
+    return cancel.transpose(0, 2, 1), beam_out
 
 
 def solution(mesh):

time: 105 us -> 83.7 us (0.80)
  Pallas kernels: 29.9 us -> 13.2 us
  local copies, waits for them, and re-layouts: 4.47 us -> 0.98 us
  other arithmetic: 1.68 us -> 0 us
    pallas_call x2 -> x3, Pallas kernels: 27.8 us -> 12.7 us  [the longest x1 9.74 us: body(): pl.pallas_call(array_kernel, out_shape=(jax.ShapeDtypeStruct((8, 2, 62),...]
    pallas_call x1, Pallas kernels: 2.1 us -> 0.49 us  [body(): pl.pallas_call(beams_kernel, out_shape=(jax.ShapeDtypeStruct((64, 256), j...]
    unnamed x10 -> x6, local copies, waits for them, and re-layouts: 1.61 us -> 0.01 us
    another operation x4 -> x0, other arithmetic: 1.5 us -> none  [the longest x1 0.79 us: steering_columns(): real = jnp.stack([cosine, -sine], axis=-1)]
  transfers between devices with their start and end apart: 2 -> 2, of which waited for: 2 -> 2; matrix products, arithmetic and copies ran while one was open for 1% -> 0% of each run, Pallas kernels for 0% -> 0%
where the time goes in v2:
time: 83.7 us; the launch traced here: 83.4 us
  blocking collectives  59.1 us (71%)
  Pallas kernels  13.2 us (16%)
  starting transfers between devices  7.32 us (9%)
  waiting for transfers between devices  2.07 us (2%)
  local copies, waits for them, and re-layouts  0.98 us (1%)
    all_to_all x1, blocking collectives, body(): got = lax.all_to_all(message, TILE, 0, 0, tiled=True)  32.7 us
    all_to_all x1, blocking collectives, body(): gathered = lax.all_to_all(lines, ('panel', 'tile_y'), 0, 0, tiled=True)  26.4 us
    pallas_call x1, Pallas kernels, body(): pl.pallas_call(array_kernel, out_shape=(jax.ShapeDtypeStruct((8, 2, 62),...  9.74 us
    ppermute x1, starting transfers between devices, body(): other = lax.ppermute(gathered, 'core', [(0, 1), (1, 0)])  3.86 us
    ppermute x1, starting transfers between devices, body(): other = lax.ppermute(covar, 'core', [(0, 1), (1, 0)])  3.45 us
    pallas_call x1, Pallas kernels, body(): pl.pallas_call(cancel_kernel, out_shape=jax.ShapeDtypeStruct((640, 128),...  2.88 us
  transfers between devices with their start and end apart: 2, of which 2 were waited for; matrix products, arithmetic and copies ran while one was open for 0% of the time, Pallas kernels for 0%

profile of v2, /device:TPU:1, one launch (start us, length us, event | category | flops | bytes accessed | tf_op | source)
XLA Modules:
  0.0 83.4 jit_solution(978269646746732249)
XLA Ops:
  0.6 0.0 copy-start
  0.6 1.0 %reshape.17.samples_ref = bf16[8,16,512]{2,1,0:T(8,128)(2,1)S(1)} reshape(bf16[8,8,2,512]{3,2,1,0:T(2,128)(2,1)} %param.4) | data formatting | bytes 262144 | tf_op jit(solution)/shard_map/reshape | solution.py:282
  1.6 0.0 copy-done
  1.6 0.1 message.1
  1.7 32.7 %all_to_all.10.got_ref = bf16[32,40,128]{2,1,0:T(8,128)(2,1)S(1)} all-to-all(bf16[32,40,128]{2,1,0:T(8,128)(2,1)S(1)} %message.1), channel_id=1, replica_groups=mesh['panel'=16,'tile_y'=8,'tile_z'=2,'core'=2] {'tile_y','tile_z','core'}, dimensions={0} | all-to-all | bytes 655360 | tf_op jit(solution)/shard_map/all_to_all | solution.py:283
  34.4 0.5 beams.1
  34.9 0.0 copy-start.1
  34.9 3.5 %collective-permute-start = (f32[64,64]{1,0:T(8,128)S(1)}, f32[64,64]{1,0:T(8,128)S(1)}, u32[]{:S(2)}, u32[]{:S(2)}) collective-permute-start(f32[64,64]{1,0:T(8,128)S(1)} %get-tuple-element.7.own_ref), channel_id=1, source_target_pairs={{0,1},{1,0},{2,3},{3,2},{4,5},{5,4},{6,7},{7,6},{8,9},{9,8},{10,11... | collective-permute-start | bytes 49160 | tf_op jit(solution)/shard_map/ppermute | solution.py:295
  38.4 0.8 %collective-permute-done.other_ref = f32[64,64]{1,0:T(8,128)S(1)} collective-permute-done((f32[64,64]{1,0:T(8,128)S(1)}, f32[64,64]{1,0:T(8,128)S(1)}, u32[]{:S(2)}, u32[]{:S(2)}) %collective-permute-start) | collective-permute-done | bytes 16416 | tf_op jit(solution)/shard_map/ppermute | solution.py:295
  39.2 0.0 copy-done.1
  39.2 2.9 %cancel.1 = f32[640,128]{1,0:T(8,128)S(1)} custom-call(f32[8]{0:T(128)S(1)} %copy-done.1, f32[64,256]{1,0:T(8,128)S(1)} %get-tuple-element.6.beams_ref, f32[64,64]{1,0:T(8,128)S(1)} %get-tuple-element.7.own_ref, f32[64,64]{1,0:T(8,128)S(1)} %collective-permute-done.other_ref), custom_call_target="tpu_custom_call" | custom-call | tf_op jit(solution)/shard_map/cancel/pallas_call | solution.py:296
  42.1 26.4 %all_to_all.11 = f32[128,5,1,128]{3,2,1,0:T(1,128)S(1)} all-to-all(f32[128,5,1,128]{3,2,1,0:T(1,128)S(1)} %bitcast.7), channel_id=1, replica_groups=mesh['panel'=16,'tile_y'=8,'tile_z'=2,'core'=2] {'panel','tile_y'}, dimensions={0} | all-to-all | bytes 655360 | tf_op jit(solution)/shard_map/all_to_all | solution.py:305
  68.6 0.0 copy-start.2
  68.6 3.9 %collective-permute-start.1 = (f32[640,128]{1,0:T(8,128)S(1)}, f32[640,128]{1,0:T(8,128)S(1)}, u32[]{:S(2)}, u32[]{:S(2)}) collective-permute-start(f32[640,128]{1,0:T(8,128)S(1)} %bitcast.5), channel_id=1, source_target_pairs={{0,1},{1,0},{2,3},{3,2},{4,5},{5,4},{6,7},{7,6},{8,9},{9,8},{10,11... | collective-permute-start | bytes 983048 | tf_op jit(solution)/shard_map/ppermute | solution.py:307
  72.4 1.2 %collective-permute-done.1.other_ref = f32[640,128]{1,0:T(8,128)S(1)} collective-permute-done((f32[640,128]{1,0:T(8,128)S(1)}, f32[640,128]{1,0:T(8,128)S(1)}, u32[]{:S(2)}, u32[]{:S(2)}) %collective-permute-start.1) | collective-permute-done | bytes 327712 | tf_op jit(solution)/shard_map/ppermute | solution.py:307
  73.7 0.0 copy-done.2
  73.7 9.7 %array.1 = (f32[8,2,62]{2,1,0:T(2,128)}, f32[2,16]{1,0:T(2,128)}) custom-call(s32[1,128]{1,0:T(1,128)S(1)} %bitcast.9, f32[640,128]{1,0:T(8,128)S(1)} %bitcast.6, f32[640,128]{1,0:T(8,128)S(1)} %collective-permute-done.1.other_ref), custom_call_target="tpu_custom_call" | custom-call | tf_op jit(solution)/shard_map/array/pallas_call | solution.py:308
Async XLA Ops:
  0.6 1.0 %copy-start = (s32[32,8]{0,1:T(8,128)S(1)}, s32[32,8]{0,1:T(8,128)}, u32[]{:S(2)}) copy-start(s32[32,8]{0,1:T(8,128)} %param.5) | copy-start | bytes 3076
  34.9 4.3 %copy-start.1 = (f32[8]{0:T(128)S(1)}, f32[8]{0:T(128)}, u32[]{:S(2)}) copy-start(f32[8]{0:T(128)} %loading_ref.1) | copy-start | bytes 100
  34.9 4.3 %collective-permute-start = (f32[64,64]{1,0:T(8,128)S(1)}, f32[64,64]{1,0:T(8,128)S(1)}, u32[]{:S(2)}, u32[]{:S(2)}) collective-permute-start(f32[64,64]{1,0:T(8,128)S(1)} %get-tuple-element.7.own_ref), channel_id=1, source_target_pairs={{0,1},{1,0},{2,3},{3,2},{4,5},{5,4},{6,7},{7,6},{8,9},{9,8},{10,11... | collective-permute-start | bytes 49160 | tf_op jit(solution)/shard_map/ppermute | solution.py:295
  68.6 5.1 %copy-start.2 = (s32[128]{0:T(128)S(1)}, s32[128]{0:T(128)}, u32[]{:S(2)}) copy-start(s32[128]{0:T(128)} %param.6) | copy-start | bytes 1540
  68.6 5.1 %collective-permute-start.1 = (f32[640,128]{1,0:T(8,128)S(1)}, f32[640,128]{1,0:T(8,128)S(1)}, u32[]{:S(2)}, u32[]{:S(2)}) collective-permute-start(f32[640,128]{1,0:T(8,128)S(1)} %bitcast.5), channel_id=1, source_target_pairs={{0,1},{1,0},{2,3},{3,2},{4,5},{5,4},{6,7},{7,6},{8,9},{9,8},{10,11... | collective-permute-start | bytes 983048 | tf_op jit(solution)/shard_map/ppermute | solution.py:307

commit v3 on v2

v3 whole, which is shorter than its diff:
```python
import math

import jax
import jax.numpy as jnp
from jax import lax
from jax.experimental import pallas as pl
from jax.experimental.pallas import tpu as pltpu
from jax.sharding import Mesh
from jax.sharding import PartitionSpec as P

SNAPS = 512
PHASE_LEVELS = 64
ARRAY_LOAD = 1.0
TILE = ("tile_y", "tile_z", "core")
CHUNK = 16
NEAR = 16
HIGHEST = lax.Precision.HIGHEST


def vmem():
    return pl.BlockSpec(memory_space=pltpu.VMEM)


def smem():
    return pl.BlockSpec(memory_space=pltpu.SMEM)


def limit(mebibytes):
    return pltpu.CompilerParams(vmem_limit_bytes=mebibytes << 20)


def lanes_of(block, lane):
    return jnp.broadcast_to(block[:, lane : lane + 1], (8, 128))


def row_of(block, row):
    return jnp.broadcast_to(block[row : row + 1, :], (8, 128))


def eliminate(rows, first_lane, steps):
    rows = [list(row) for row in rows]
    place = lax.broadcasted_iota(jnp.int32, (8, 128), 0)
    for first in range(0, steps, CHUNK):
        count = min(CHUNK, steps - first)
        spread = [[lanes_of(row[0], first_lane + first + u) for u in range(count)] for row in rows]
        for t in range(count):
            own, s = divmod(first + t, 8)
            scale = 1.0 / row_of(spread[own][t], s)
            lead = {u: row_of(spread[own][u], s) for u in range(t + 1, count)}
            upper = [row_of(group, s) for group in rows[own]]
            for i, row in enumerate(rows):
                f = spread[i][t]
                if i == own:
                    for u in lead:
                        line = lead[u] * scale
                        if u == t + 1:
                            value = spread[i][u] - (f * lead[u]) * scale
                        else:
                            value = spread[i][u] - f * line
                        spread[i][u] = jnp.where(place == s, line, value)
                    for g in range(len(row)):
                        line = upper[g] * scale
                        row[g] = jnp.where(place == s, line, row[g] - f * line)
                else:
                    f = f * scale
                    for u in lead:
                        spread[i][u] = spread[i][u] - f * lead[u]
                    for g in range(len(row)):
                        row[g] = row[g] - f * upper[g]
    return rows


def less_product(value, spread, lines):
    terms = [f * line for f, line in zip(spread, lines)]
    while len(terms) > 1:
        terms = [sum(terms[i : i + 2]) for i in range(0, len(terms), 2)]
    return value - terms[0]


def forward(rows, steps):
    rows = [list(row) for row in rows]
    for first in range(0, steps, CHUNK):
        count = min(CHUNK, steps - first)
        own = range(first // 8, (first + count + 7) // 8)
        below = range(own.stop, len(rows))
        spread = {i: [lanes_of(rows[i][0], first + t) for t in range(count)] for i in below}
        solved = eliminate([rows[i] for i in own], first, count)
        for i, row in zip(own, solved):
            rows[i] = row
        for g in range(len(rows[0])):
            lines = [row_of(solved[t // 8][g], t % 8) for t in range(count)]
            for i in below:
                rows[i][g] = less_product(rows[i][g], spread[i], lines)
    return rows


def cosine_of(steps):
    quarter = (steps + 8) >> 4
    angle = (steps - 16 * quarter).astype(jnp.float32) * (2.0 * math.pi / PHASE_LEVELS)
    square = angle * angle
    cosine = 1.0 + square * (
        -1 / 2 + square * (1 / 24 + square * (-1 / 720 + square * (1 / 40320 - square / 3628800)))
    )
    sine = angle * (
        1.0 + square * (-1 / 6 + square * (1 / 120 + square * (-1 / 5040 + square / 362880)))
    )
    value = jnp.where((quarter & 1) == 0, cosine, sine)
    return jnp.where(((quarter + 1) & 2) == 0, value, -value)


def message_kernel(samples_ref, codes_ref, out_ref):
    codes = jnp.concatenate([codes_ref[...], jnp.zeros((8, 96), jnp.int32)], axis=1)
    row = lax.broadcasted_iota(jnp.int32, (8, 128), 0)
    lane = lax.broadcasted_iota(jnp.int32, (8, 128), 1)
    real = pltpu.roll(codes, 127, 1)
    imag = pltpu.roll(codes, 30, 1)
    last = pltpu.roll(codes, 62, 1)
    twin = pltpu.roll(codes, 63, 1)
    codes = jnp.where(lane < 31, real, jnp.where(lane < 62, imag, last))
    codes = jnp.where(lane == 63, twin, codes)
    imaginary = jnp.where((lane >= 31) & (lane != 62), 1, 0)

    def columns(first):
        spread = row_of(codes, first)
        for t in range(1, 4):
            spread = jnp.where(row >= 2 * t, row_of(codes, first + t), spread)
        return cosine_of(spread + 16 * (imaginary - (row & 1)))

    table = jnp.concatenate([columns(0), columns(4)], axis=0)
    table = (table / math.sqrt(256)).astype(jnp.bfloat16)
    for p in range(8):
        for z in range(2):
            for b in range(4):
                out_ref[2 * p + z, 16 * b : 16 * b + 16, :] = samples_ref[
                    p, :, 128 * b : 128 * b + 128
                ]
            out_ref[2 * p + z, 64:80, :] = table


def beams_kernel(got_ref, beams_ref):
    got = got_ref[...]
    table = got[:, 64:80, :].reshape(256, 128)
    samples = jnp.concatenate(
        [got[:, 16 * b : 16 * b + 16, :].reshape(256, 128) for b in range(4)], axis=1
    )
    beams_ref[...] = lax.dot_general(
        table, samples, (((0,), (0,)), ((), ())), preferred_element_type=jnp.float32
    )[:64]


def cancel_kernel(loading_ref, own_ref, other_ref, out_ref):
    load = loading_ref[lax.axis_index("tile_y")]
    core = lax.axis_index("core")
    beams = own_ref[...] + other_ref[...]
    covar = square(beams) / SNAPS
    row = lax.broadcasted_iota(jnp.int32, (64, 64), 0)
    column = lax.broadcasted_iota(jnp.int32, (64, 64), 1)
    covar = covar + jnp.where(row == column, load, 0.0)
    covar = jnp.concatenate([covar, jnp.zeros((64, 64), jnp.float32)], axis=1)
    half = jnp.where(core == 0, beams[:, :256], beams[:, 256:])
    row = lax.broadcasted_iota(jnp.int32, (64, 128), 0)
    column = lax.broadcasted_iota(jnp.int32, (64, 128), 1) & 63
    source = jnp.where(column < 62, column // 2 + 31 * (column & 1), 64)
    identity = jnp.where(row == source, 1.0, 0.0)
    whole = jnp.concatenate([covar, half, identity], axis=1)
    rows = [
        [whole[8 * i : 8 * i + 8, 128 * g : 128 * g + 128] for g in range(4)] for i in range(8)
    ]
    last = forward(rows, 62)[7]
    lane = lax.broadcasted_iota(jnp.int32, (1, 128), 1)
    cancel = jnp.where(lane < 64, -last[3][6:7, :], -last[3][7:8, :])
    line = jnp.concatenate([last[1][6:8, :], last[2][6:8, :], cancel], axis=0)
    for i in range(8):
        out_ref[5 * i : 5 * i + 5, :] = line
    lines = out_ref[0:40, :]
    for i in range(1, 16):
        out_ref[40 * i : 40 * i + 40, :] = lines


def square(value):
    return lax.dot_general(
        value,
        value,
        (((1,), (1,)), ((), ())),
        precision=HIGHEST,
        preferred_element_type=jnp.float32,
    )


def flat_half(ref):
    return jnp.concatenate(
        [
            jnp.concatenate(
                [ref[pl.ds(2 * b + k, 128, stride=5), :] for b in range(2)], axis=1
            )
            for k in range(2)
        ],
        axis=0,
    )


def own_columns(flat, half):
    y = lax.axis_index("tile_y")
    slot = (y % 2) * 4 + lax.axis_index("tile_z") * 2 + lax.axis_index("core")
    mine = jnp.where((y % 4) // 2 == 0, flat[:, :128], flat[:, 128:])
    mine = pltpu.roll(mine, lax.rem(128 - 16 * slot, 128), 1)
    lane = lax.broadcasted_iota(jnp.int32, (256, 128), 1)
    return jnp.where((lane < 16) & (half == y // 4), mine, 0.0)


def own_kernel(codes_ref, own_ref, cancel_ref, out_ref):
    cancel = own_ref[pl.ds(lax.axis_index("panel") * 40 + 4, 8, stride=5), :]
    cancel_ref[:, 0, :] = cancel[:, :62]
    cancel_ref[:, 1, :] = pltpu.roll(cancel, 64, 1)[:, :62]
    own = flat_half(own_ref)
    row = lax.broadcasted_iota(jnp.int32, (256, 256), 0)
    column = lax.broadcasted_iota(jnp.int32, (256, 256), 1)
    out_ref[0:256, 0:256] = square(own) / SNAPS + jnp.where(row == column, ARRAY_LOAD, 0.0)
    cosine = cosine_of(codes_ref[...])
    sine = cosine_of(codes_ref[...] - 16)
    spread_cosine = jnp.broadcast_to(cosine, (128, 128)).T
    spread_sine = jnp.broadcast_to(sine, (128, 128)).T
    mine = own_columns(own, lax.axis_index("core"))
    lane = lax.broadcasted_iota(jnp.int32, (128, 128), 1)

    def right_side(values, first, second):
        return jnp.where(lane == 16, first, jnp.where(lane == 17, second, values))

    out_ref[0:128, 256:384] = right_side(mine[:128], spread_cosine, -spread_sine)
    out_ref[128:256, 256:384] = right_side(mine[128:], spread_sine, spread_cosine)
    out_ref[256:264, :] = jnp.zeros((8, 384), jnp.float32)
    out_ref[256:257, 0:128] = cosine
    out_ref[256:257, 128:256] = sine
    out_ref[257:258, 0:128] = -sine
    out_ref[257:258, 128:256] = cosine


def array_kernel(start_ref, other_ref, out_ref, work_ref):
    other = flat_half(other_ref)
    work_ref[0:256, 0:256] = start_ref[0:256, 0:256] + square(other) / SNAPS
    work_ref[0:256, 256:384] = start_ref[0:256, 256:384] + own_columns(
        other, 1 - lax.axis_index("core")
    )
    work_ref[256:264, :] = start_ref[256:264, :]

    for base in range(0, 256, CHUNK):
        stop = base + CHUNK
        first = base // 128
        lane = base % 128
        groups = list(range(first, 3))
        after = list(range(stop // 128, 3))
        near = min(stop + NEAR, 264) if stop < 256 else 264
        rows = [
            [work_ref[r : r + 8, 128 * g : 128 * g + 128] for g in groups]
            for r in range(base, stop, 8)
        ]
        spread = {
            r: [
                lanes_of(work_ref[r : r + 8, 128 * first : 128 * first + 128], lane + t)
                for t in range(CHUNK)
            ]
            for r in range(stop, near, 8)
        }
        rows = eliminate(rows, lane, CHUNK)
        rows = [[row[g - first] for g in after] for row in rows]
        for i, g in enumerate(after):
            lines = [row_of(rows[t // 8][i], t % 8) for t in range(CHUNK)]
            span = slice(128 * g, 128 * g + 128)
            for r in range(stop, near, 8):
                work_ref[r : r + 8, span] = less_product(work_ref[r : r + 8, span], spread[r], lines)
        if near < 264:
            left = 128 * after[0]
            parts = [jnp.concatenate(row, axis=1) for row in rows]
            if lane:
                parts = [jnp.zeros((lane, 384 - left), jnp.float32)] + parts
            if lane + CHUNK < 128:
                parts = parts + [jnp.zeros((128 - lane - CHUNK, 384 - left), jnp.float32)]
            factor = work_ref[near:264, 128 * first : 128 * first + 128]
            work_ref[near:264, left:384] = work_ref[near:264, left:384] - jnp.dot(
                factor,
                jnp.concatenate(parts, axis=0),
                precision=HIGHEST,
                preferred_element_type=jnp.float32,
            )

    final = -work_ref[256:264, 256:384]
    upper = row_of(final, 0)
    lower = row_of(final, 1)
    g00 = lanes_of(upper, 16)
    g01 = lanes_of(upper, 17)
    g10 = lanes_of(lower, 16)
    g11 = lanes_of(lower, 17)
    scale = math.sqrt(128.0) / (g00 * g11 - g01 * g10)
    first_row = (g11 * upper - g10 * lower) * scale
    second_row = (g00 * lower - g01 * upper) * scale
    place = lax.broadcasted_iota(jnp.int32, (8, 128), 0)
    out_ref[...] = jnp.where(place == 0, first_row, second_row)[0:2, 0:16]


def body(snapshots, beam_codes, panel_codes, loading):
    message = pl.pallas_call(
        message_kernel,
        out_shape=jax.ShapeDtypeStruct((16, 80, 128), jnp.bfloat16),
        in_specs=[vmem(), vmem()],
        out_specs=vmem(),
        compiler_params=limit(4),
        name="message",
    )(snapshots.reshape(8, 16, SNAPS), beam_codes.T)
    got = lax.all_to_all(message, ("tile_y", "tile_z"), 0, 0, tiled=True)
    beams = pl.pallas_call(
        beams_kernel,
        out_shape=jax.ShapeDtypeStruct((64, SNAPS), jnp.float32),
        in_specs=[vmem()],
        out_specs=vmem(),
        compiler_params=limit(4),
        name="beams",
    )(got)
    other = lax.ppermute(beams, "core", [(0, 1), (1, 0)])
    lines = pl.pallas_call(
        cancel_kernel,
        out_shape=jax.ShapeDtypeStruct((640, 128), jnp.float32),
        in_specs=[smem(), vmem(), vmem()],
        out_specs=vmem(),
        compiler_params=limit(4),
        name="cancel",
    )(loading, beams, other)
    lines = lines.reshape(128, 5, 1, 128)
    gathered = lax.all_to_all(lines, ("panel", "tile_y"), 0, 0, tiled=True)
    gathered = gathered.reshape(640, 128)
    other = lax.ppermute(gathered, "core", [(0, 1), (1, 0)])
    cancel, start = pl.pallas_call(
        own_kernel,
        out_shape=(
            jax.ShapeDtypeStruct((8, 2, 62), jnp.float32),
            jax.ShapeDtypeStruct((264, 384), jnp.float32),
        ),
        in_specs=[vmem(), vmem()],
        out_specs=(vmem(), vmem()),
        compiler_params=limit(8),
        cost_estimate=pl.CostEstimate(flops=400000000, bytes_accessed=800000, transcendentals=0),
        name="own",
    )(panel_codes.reshape(1, 128), gathered)
    beam_out = pl.pallas_call(
        array_kernel,
        out_shape=jax.ShapeDtypeStruct((2, 16), jnp.float32),
        in_specs=[vmem(), vmem()],
        out_specs=vmem(),
        scratch_shapes=[pltpu.VMEM((264, 384), jnp.float32)],
        compiler_params=limit(8),
        name="array",
    )(start, other)
    return cancel.transpose(0, 2, 1), beam_out


def solution(mesh):
    torus = Mesh(
        mesh.devices.reshape(mesh.shape["panel"], 8, 2, 2), ("panel", "tile_y", "tile_z", "core")
    )
    return jax.shard_map(
        body,
        mesh=torus,
        in_specs=(P("panel", TILE, None, None), P(None, TILE), P(), P("panel")),
        out_specs=(P("panel", None, None), P(None, TILE)),
        check_vma=False,
    )
```

time: 83.7 us -> 80.7 us (0.964)
  Pallas kernels: 13.2 us -> 11.3 us
  blocking collectives: 59.1 us -> 58.1 us
    pallas_call x3 -> x4, Pallas kernels: 10.3 us -> 8.88 us  [the longest x1 7.7 us: body(): pl.pallas_call(array_kernel, out_shape=jax.ShapeDtypeStruct((2, 16), jnp....]
    ppermute x1, waiting for transfers between devices: 1.23 us -> 0.35 us  [body(): other = lax.ppermute(gathered, 'core', [(0, 1), (1, 0)])]
  transfers between devices with their start and end apart: 2 -> 2, of which waited for: 2 -> 2; matrix products, arithmetic and copies ran while one was open for 0% -> 0% of each run, Pallas kernels for 0% -> 1%
where the time goes in v3:
time: 80.7 us; the launch traced here: 80.5 us
  blocking collectives  58.1 us (72%)
  Pallas kernels  11.3 us (14%)
  starting transfers between devices  7.99 us (10%)
  waiting for transfers between devices  1.31 us (2%)
  local copies, waits for them, and re-layouts  0.98 us (1%)
    all_to_all x1, blocking collectives, body(): got = lax.all_to_all(message, ('tile_y', 'tile_z'), 0, 0, tiled=True)  32 us
    all_to_all x1, blocking collectives, body(): gathered = lax.all_to_all(lines, ('panel', 'tile_y'), 0, 0, tiled=True)  26.2 us
    pallas_call x1, Pallas kernels, body(): pl.pallas_call(array_kernel, out_shape=jax.ShapeDtypeStruct((2, 16), jnp....  7.7 us
    ppermute x1, starting transfers between devices, body(): other = lax.ppermute(beams, 'core', [(0, 1), (1, 0)])  4.12 us
    ppermute x1, starting transfers between devices, body(): other = lax.ppermute(gathered, 'core', [(0, 1), (1, 0)])  3.87 us
    pallas_call x1, Pallas kernels, body(): pl.pallas_call(cancel_kernel, out_shape=jax.ShapeDtypeStruct((640, 128),...  2.46 us
  transfers between devices with their start and end apart: 2, of which 2 were waited for; matrix products, arithmetic and copies ran while one was open for 0% of the time, Pallas kernels for 1%

profile of v3, /device:TPU:1, one launch (start us, length us, event | category | flops | bytes accessed | tf_op | source)
XLA Modules:
  0.0 80.5 jit_solution(542819850476057544)
XLA Ops:
  0.6 0.0 copy-start
  0.6 1.0 %reshape.17.samples_ref = bf16[8,16,512]{2,1,0:T(8,128)(2,1)S(1)} reshape(bf16[8,8,2,512]{3,2,1,0:T(2,128)(2,1)} %param.4) | data formatting | bytes 262144 | tf_op jit(solution)/shard_map/reshape | solution.py:308
  1.6 0.0 copy-done
  1.6 0.1 message.1
  1.7 32.0 %all_to_all.10.got_ref = bf16[16,80,128]{2,1,0:T(8,128)(2,1)S(1)} all-to-all(bf16[16,80,128]{2,1,0:T(8,128)(2,1)S(1)} %message.1), channel_id=1, replica_groups=mesh['panel'=16,'tile_y'=8,'tile_z'=2,'core'=2] {'tile_y','tile_z'}, dimensions={0} | all-to-all | bytes 655360 | tf_op jit(solution)/shard_map/all_to_all | solution.py:309
  33.7 0.0 copy-start.1
  33.7 0.2 beams.1.own_ref
  33.9 4.1 %collective-permute-start = (f32[64,512]{1,0:T(8,128)S(1)}, f32[64,512]{1,0:T(8,128)S(1)}, u32[]{:S(2)}, u32[]{:S(2)}) collective-permute-start(f32[64,512]{1,0:T(8,128)S(1)} %beams.1.own_ref), channel_id=1, source_target_pairs={{0,1},{1,0},{2,3},{3,2},{4,5},{5,4},{6,7},{7,6},{8,9},{9,8},{10,11... | collective-permute-start | bytes 393224 | tf_op jit(solution)/shard_map/ppermute | solution.py:318
  38.0 1.0 %collective-permute-done.other_ref = f32[64,512]{1,0:T(8,128)S(1)} collective-permute-done((f32[64,512]{1,0:T(8,128)S(1)}, f32[64,512]{1,0:T(8,128)S(1)}, u32[]{:S(2)}, u32[]{:S(2)}) %collective-permute-start) | collective-permute-done | bytes 131104 | tf_op jit(solution)/shard_map/ppermute | solution.py:318
  39.0 0.0 copy-done.1
  39.0 2.5 %cancel.1 = f32[640,128]{1,0:T(8,128)S(1)} custom-call(f32[8]{0:T(128)S(1)} %copy-done.1, f32[64,512]{1,0:T(8,128)S(1)} %beams.1.own_ref, f32[64,512]{1,0:T(8,128)S(1)} %collective-permute-done.other_ref), custom_call_target="tpu_custom_call" | custom-call | tf_op jit(solution)/shard_map/cancel/pallas_call | solution.py:319
  41.5 26.2 %all_to_all.11 = f32[128,5,1,128]{3,2,1,0:T(1,128)S(1)} all-to-all(f32[128,5,1,128]{3,2,1,0:T(1,128)S(1)} %bitcast.5), channel_id=1, replica_groups=mesh['panel'=16,'tile_y'=8,'tile_z'=2,'core'=2] {'panel','tile_y'}, dimensions={0} | all-to-all | bytes 655360 | tf_op jit(solution)/shard_map/all_to_all | solution.py:328
  67.6 0.0 copy-start.2
  67.6 3.9 %collective-permute-start.1 = (f32[640,128]{1,0:T(8,128)S(1)}, f32[640,128]{1,0:T(8,128)S(1)}, u32[]{:S(2)}, u32[]{:S(2)}) collective-permute-start(f32[640,128]{1,0:T(8,128)S(1)} %bitcast.6), channel_id=1, source_target_pairs={{0,1},{1,0},{2,3},{3,2},{4,5},{5,4},{6,7},{7,6},{8,9},{9,8},{10,11... | collective-permute-start | bytes 983048 | tf_op jit(solution)/shard_map/ppermute | solution.py:330
  71.5 0.0 copy-done.2
  71.5 0.9 %own.1 = (f32[8,2,62]{2,1,0:T(2,128)}, f32[264,384]{1,0:T(8,128)S(1)}) custom-call(s32[1,128]{1,0:T(1,128)S(1)} %bitcast.9, f32[640,128]{1,0:T(8,128)S(1)} %bitcast.7), custom_call_target="tpu_custom_call" | custom-call | flops 400000000 | bytes 800000 | tf_op jit(solution)/shard_map/own/pallas_call | solution.py:331
  72.4 0.3 collective-permute-done.1.other_ref
  72.8 7.7 %array.1 = f32[2,16]{1,0:T(2,128)} custom-call(f32[264,384]{1,0:T(8,128)S(1)} %get-tuple-element.5.start_ref, f32[640,128]{1,0:T(8,128)S(1)} %collective-permute-done.1.other_ref), custom_call_target="tpu_custom_call" | custom-call | tf_op jit(solution)/shard_map/array/pallas_call | solution.py:343
Async XLA Ops:
  0.6 1.0 %copy-start = (s32[32,8]{0,1:T(8,128)S(1)}, s32[32,8]{0,1:T(8,128)}, u32[]{:S(2)}) copy-start(s32[32,8]{0,1:T(8,128)} %param.5) | copy-start | bytes 3076
  33.7 5.3 %copy-start.1 = (f32[8]{0:T(128)S(1)}, f32[8]{0:T(128)}, u32[]{:S(2)}) copy-start(f32[8]{0:T(128)} %loading_ref.1) | copy-start | bytes 100
  33.9 5.1 %collective-permute-start = (f32[64,512]{1,0:T(8,128)S(1)}, f32[64,512]{1,0:T(8,128)S(1)}, u32[]{:S(2)}, u32[]{:S(2)}) collective-permute-start(f32[64,512]{1,0:T(8,128)S(1)} %beams.1.own_ref), channel_id=1, source_target_pairs={{0,1},{1,0},{2,3},{3,2},{4,5},{5,4},{6,7},{7,6},{8,9},{9,8},{10,11... | collective-permute-start | bytes 393224 | tf_op jit(solution)/shard_map/ppermute | solution.py:318
  67.6 3.9 %copy-start.2 = (s32[128]{0:T(128)S(1)}, s32[128]{0:T(128)}, u32[]{:S(2)}) copy-start(s32[128]{0:T(128)} %param.6) | copy-start | bytes 1540
  67.6 5.1 %collective-permute-start.1 = (f32[640,128]{1,0:T(8,128)S(1)}, f32[640,128]{1,0:T(8,128)S(1)}, u32[]{:S(2)}, u32[]{:S(2)}) collective-permute-start(f32[640,128]{1,0:T(8,128)S(1)} %bitcast.6), channel_id=1, source_target_pairs={{0,1},{1,0},{2,3},{3,2},{4,5},{5,4},{6,7},{7,6},{8,9},{9,8},{10,11... | collective-permute-start | bytes 983048 | tf_op jit(solution)/shard_map/ppermute | solution.py:330

commit v4 on v3

--- a/solution.py
+++ b/solution.py
@@ -14,6 +14,8 @@
 TILE = ("tile_y", "tile_z", "core")
 CHUNK = 16
 NEAR = 16
+MOVE = 32
+ROWS = 272
 HIGHEST = lax.Precision.HIGHEST
 
 
@@ -40,34 +42,64 @@
 def eliminate(rows, first_lane, steps):
     rows = [list(row) for row in rows]
     place = lax.broadcasted_iota(jnp.int32, (8, 128), 0)
-    for first in range(0, steps, CHUNK):
-        count = min(CHUNK, steps - first)
-        spread = [[lanes_of(row[0], first_lane + first + u) for u in range(count)] for row in rows]
-        for t in range(count):
-            own, s = divmod(first + t, 8)
-            scale = 1.0 / row_of(spread[own][t], s)
-            lead = {u: row_of(spread[own][u], s) for u in range(t + 1, count)}
-            upper = [row_of(group, s) for group in rows[own]]
-            for i, row in enumerate(rows):
-                f = spread[i][t]
-                if i == own:
-                    for u in lead:
-                        line = lead[u] * scale
-                        if u == t + 1:
-                            value = spread[i][u] - (f * lead[u]) * scale
-                        else:
-                            value = spread[i][u] - f * line
-                        spread[i][u] = jnp.where(place == s, line, value)
-                    for g in range(len(row)):
-                        line = upper[g] * scale
-                        row[g] = jnp.where(place == s, line, row[g] - f * line)
-                else:
-                    f = f * scale
-                    for u in lead:
-                        spread[i][u] = spread[i][u] - f * lead[u]
-                    for g in range(len(row)):
-                        row[g] = row[g] - f * upper[g]
-    return rows
+    spread = [[lanes_of(row[0], first_lane + u) for u in range(steps)] for row in rows]
+    same = [jnp.ones((8, 128), jnp.float32) for row in rows]
+    twin = [jnp.zeros((8, 128), jnp.float32) for row in rows]
+    for t in range(0, steps, 2):
+        own, s = divmod(t, 8)
+        a = row_of(spread[own][t], s)
+        b = row_of(spread[own][t + 1], s)
+        c = row_of(spread[own][t + 1], s + 1)
+        scale = 1.0 / (a * c - b * b)
+        raw = (a, b, c)
+        a, b, c = a * scale, b * scale, c * scale
+        pair = (place == s) | (place == s + 1)
+        same[own] = jnp.where(place == s, c, jnp.where(place == s + 1, a, same[own]))
+        twin[own] = jnp.where(pair, -b, twin[own])
+        first = [c * row[t] - b * row[t + 1] for row in spread]
+        second = [a * row[t + 1] - b * row[t] for row in spread]
+        first[own] = jnp.where(pair, 0.0, first[own])
+        second[own] = jnp.where(pair, 0.0, second[own])
+
+        def reduce(blocks):
+            upper = row_of(blocks[own], s)
+            lower = row_of(blocks[own], s + 1)
+            return [
+                block - (f * upper + h * lower) for block, f, h in zip(blocks, first, second)
+            ]
+
+        for u in range(t + 2, steps):
+            quick = None
+            if u < t + 4:
+                target = (t + 2) // 8
+                upper = row_of(spread[own][u], s)
+                lower = row_of(spread[own][u], s + 1)
+                block = spread[target]
+                f = raw[2] * block[t] - raw[1] * block[t + 1]
+                h = raw[0] * block[t + 1] - raw[1] * block[t]
+                change = f * upper + h * lower
+                if target == own:
+                    change = jnp.where(pair, 0.0, change)
+                quick = block[u] - change * scale
+            for row, value in zip(spread, reduce([row[u] for row in spread])):
+                row[u] = value
+            if quick is not None:
+                spread[target][u] = quick
+        for g in range(len(rows[0])):
+            for row, value in zip(rows, reduce([row[g] for row in rows])):
+                row[g] = value
+
+    def scaled(value, i):
+        lines = [row_of(value, s ^ 1) for s in range(8)]
+        for step in (1, 2, 4):
+            lines = [
+                jnp.where((place & step) == 0, lines[2 * j], lines[2 * j + 1])
+                for j in range(len(lines) // 2)
+            ]
+        swapped = lines[0]
+        return value * same[i] + swapped * twin[i]
+
+    return [[scaled(value, i) for value in row] for i, row in enumerate(rows)]
 
 
 def less_product(value, spread, lines):
@@ -235,6 +267,42 @@
     out_ref[257:258, 128:256] = cosine
 
 
+def split(value):
+    high = value.astype(jnp.bfloat16)
+    rest = value - high.astype(jnp.float32)
+    middle = rest.astype(jnp.bfloat16)
+    low = (rest - middle.astype(jnp.float32)).astype(jnp.bfloat16)
+    return high, middle, low
+
+
+def product(factor, solved, lane):
+    width = solved.shape[1]
+
+    def placed(part):
+        parts = [part]
+        if lane:
+            parts = [jnp.zeros((lane, width), jnp.bfloat16)] + parts
+        if lane + CHUNK < 128:
+            parts = parts + [jnp.zeros((128 - lane - CHUNK, width), jnp.bfloat16)]
+        return jnp.concatenate(parts, axis=0)
+
+    high, middle, low = split(factor)
+    upper, centre, lower = [placed(part) for part in split(solved)]
+
+    def multiplied(left, right):
+        return jnp.dot(
+            jnp.concatenate(left, axis=1),
+            jnp.concatenate(right, axis=0),
+            preferred_element_type=jnp.float32,
+        )
+
+    return (
+        multiplied((high, low), (lower, upper))
+        + multiplied((high, middle), (centre, centre))
+        + multiplied((high, middle), (upper, upper))
+    )
+
+
 def array_kernel(start_ref, other_ref, out_ref, work_ref):
     other = flat_half(other_ref)
     work_ref[0:256, 0:256] = start_ref[0:256, 0:256] + square(other) / SNAPS
@@ -242,14 +310,15 @@
         other, 1 - lax.axis_index("core")
     )
     work_ref[256:264, :] = start_ref[256:264, :]
+    work_ref[264:272, :] = jnp.zeros((8, 384), jnp.float32)
 
     for base in range(0, 256, CHUNK):
         stop = base + CHUNK
         first = base // 128
         lane = base % 128
-        groups = list(range(first, 3))
-        after = list(range(stop // 128, 3))
-        near = min(stop + NEAR, 264) if stop < 256 else 264
+        groups = [0, 1, 2] if base < MOVE else [first, 1 - first]
+        after = [g for g in groups if base < MOVE or g == 0 or stop < 256]
+        near = min(stop + NEAR, ROWS) if stop < 256 else 264
         rows = [
             [work_ref[r : r + 8, 128 * g : 128 * g + 128] for g in groups]
             for r in range(base, stop, 8)
@@ -262,28 +331,27 @@
             for r in range(stop, near, 8)
         }
         rows = eliminate(rows, lane, CHUNK)
-        rows = [[row[g - first] for g in after] for row in rows]
+        rows = [[row[groups.index(g)] for g in after] for row in rows]
         for i, g in enumerate(after):
             lines = [row_of(rows[t // 8][i], t % 8) for t in range(CHUNK)]
             span = slice(128 * g, 128 * g + 128)
             for r in range(stop, near, 8):
                 work_ref[r : r + 8, span] = less_product(work_ref[r : r + 8, span], spread[r], lines)
-        if near < 264:
-            left = 128 * after[0]
-            parts = [jnp.concatenate(row, axis=1) for row in rows]
-            if lane:
-                parts = [jnp.zeros((lane, 384 - left), jnp.float32)] + parts
-            if lane + CHUNK < 128:
-                parts = parts + [jnp.zeros((128 - lane - CHUNK, 384 - left), jnp.float32)]
-            factor = work_ref[near:264, 128 * first : 128 * first + 128]
-            work_ref[near:264, left:384] = work_ref[near:264, left:384] - jnp.dot(
-                factor,
-                jnp.concatenate(parts, axis=0),
-                precision=HIGHEST,
-                preferred_element_type=jnp.float32,
-            )
-
-    final = -work_ref[256:264, 256:384]
+        if near < ROWS:
+            factor = work_ref[near:ROWS, 128 * first : 128 * first + 128]
+            solved = jnp.concatenate([jnp.concatenate(row, axis=1) for row in rows], axis=0)
+            delta = product(factor, solved, lane)
+            for i, g in enumerate(after):
+                span = slice(128 * g, 128 * g + 128)
+                work_ref[near:ROWS, span] = work_ref[near:ROWS, span] - delta[:, 128 * i : 128 * i + 128]
+        if stop == MOVE:
+            moved = lax.broadcasted_iota(jnp.int32, (8, 128), 1) < 18
+            for r in range(stop, ROWS, 8):
+                work_ref[r : r + 8, 0:128] = jnp.where(
+                    moved, work_ref[r : r + 8, 256:384], work_ref[r : r + 8, 0:128]
+                )
+
+    final = -work_ref[256:264, 0:128]
     upper = row_of(final, 0)
     lower = row_of(final, 1)
     g00 = lanes_of(upper, 16)
@@ -345,7 +413,7 @@
         out_shape=jax.ShapeDtypeStruct((2, 16), jnp.float32),
         in_specs=[vmem(), vmem()],
         out_specs=vmem(),
-        scratch_shapes=[pltpu.VMEM((264, 384), jnp.float32)],
+        scratch_shapes=[pltpu.VMEM((ROWS, 384), jnp.float32)],
         compiler_params=limit(8),
         name="array",
     )(start, other)

time: 80.7 us -> 79.9 us (0.990)
  no operation moved by 1% of the time
where the time goes in v4:
time: 79.9 us; the launch traced here: 79.7 us
  blocking collectives  58.1 us (73%)
  Pallas kernels  10.6 us (13%)
  starting transfers between devices  7.99 us (10%)
  waiting for transfers between devices  1.31 us (2%)
  local copies, waits for them, and re-layouts  0.98 us (1%)
    all_to_all x1, blocking collectives, body(): got = lax.all_to_all(message, ('tile_y', 'tile_z'), 0, 0, tiled=True)  32 us
    all_to_all x1, blocking collectives, body(): gathered = lax.all_to_all(lines, ('panel', 'tile_y'), 0, 0, tiled=True)  26.2 us
    pallas_call x1, Pallas kernels, body(): pl.pallas_call(array_kernel, out_shape=jax.ShapeDtypeStruct((2, 16), jnp....  7.08 us
    ppermute x1, starting transfers between devices, body(): other = lax.ppermute(beams, 'core', [(0, 1), (1, 0)])  4.12 us
    ppermute x1, starting transfers between devices, body(): other = lax.ppermute(gathered, 'core', [(0, 1), (1, 0)])  3.87 us
    pallas_call x1, Pallas kernels, body(): pl.pallas_call(cancel_kernel, out_shape=jax.ShapeDtypeStruct((640, 128),...  2.32 us
  transfers between devices with their start and end apart: 2, of which 2 were waited for; matrix products, arithmetic and copies ran while one was open for 0% of the time, Pallas kernels for 1%

profile of v4, /device:TPU:1, one launch (start us, length us, event | category | flops | bytes accessed | tf_op | source)
XLA Modules:
  0.0 79.7 jit_solution(3448761878636801136)
XLA Ops:
  0.6 0.0 copy-start
  0.6 1.0 %reshape.17.samples_ref = bf16[8,16,512]{2,1,0:T(8,128)(2,1)S(1)} reshape(bf16[8,8,2,512]{3,2,1,0:T(2,128)(2,1)} %param.4) | data formatting | bytes 262144 | tf_op jit(solution)/shard_map/reshape | solution.py:376
  1.6 0.0 copy-done
  1.6 0.1 message.1
  1.7 32.0 %all_to_all.10.got_ref = bf16[16,80,128]{2,1,0:T(8,128)(2,1)S(1)} all-to-all(bf16[16,80,128]{2,1,0:T(8,128)(2,1)S(1)} %message.1), channel_id=1, replica_groups=mesh['panel'=16,'tile_y'=8,'tile_z'=2,'core'=2] {'tile_y','tile_z'}, dimensions={0} | all-to-all | bytes 655360 | tf_op jit(solution)/shard_map/all_to_all | solution.py:377
  33.7 0.0 copy-start.1
  33.7 0.2 beams.1.own_ref
  33.9 4.1 %collective-permute-start = (f32[64,512]{1,0:T(8,128)S(1)}, f32[64,512]{1,0:T(8,128)S(1)}, u32[]{:S(2)}, u32[]{:S(2)}) collective-permute-start(f32[64,512]{1,0:T(8,128)S(1)} %beams.1.own_ref), channel_id=1, source_target_pairs={{0,1},{1,0},{2,3},{3,2},{4,5},{5,4},{6,7},{7,6},{8,9},{9,8},{10,11... | collective-permute-start | bytes 393224 | tf_op jit(solution)/shard_map/ppermute | solution.py:386
  38.0 1.0 %collective-permute-done.other_ref = f32[64,512]{1,0:T(8,128)S(1)} collective-permute-done((f32[64,512]{1,0:T(8,128)S(1)}, f32[64,512]{1,0:T(8,128)S(1)}, u32[]{:S(2)}, u32[]{:S(2)}) %collective-permute-start) | collective-permute-done | bytes 131104 | tf_op jit(solution)/shard_map/ppermute | solution.py:386
  39.0 0.0 copy-done.1
  39.0 2.3 %cancel.1 = f32[640,128]{1,0:T(8,128)S(1)} custom-call(f32[8]{0:T(128)S(1)} %copy-done.1, f32[64,512]{1,0:T(8,128)S(1)} %beams.1.own_ref, f32[64,512]{1,0:T(8,128)S(1)} %collective-permute-done.other_ref), custom_call_target="tpu_custom_call" | custom-call | tf_op jit(solution)/shard_map/cancel/pallas_call | solution.py:387
  41.3 26.2 %all_to_all.11 = f32[128,5,1,128]{3,2,1,0:T(1,128)S(1)} all-to-all(f32[128,5,1,128]{3,2,1,0:T(1,128)S(1)} %bitcast.5), channel_id=1, replica_groups=mesh['panel'=16,'tile_y'=8,'tile_z'=2,'core'=2] {'panel','tile_y'}, dimensions={0} | all-to-all | bytes 655360 | tf_op jit(solution)/shard_map/all_to_all | solution.py:396
  67.5 0.0 copy-start.2
  67.5 3.9 %collective-permute-start.1 = (f32[640,128]{1,0:T(8,128)S(1)}, f32[640,128]{1,0:T(8,128)S(1)}, u32[]{:S(2)}, u32[]{:S(2)}) collective-permute-start(f32[640,128]{1,0:T(8,128)S(1)} %bitcast.6), channel_id=1, source_target_pairs={{0,1},{1,0},{2,3},{3,2},{4,5},{5,4},{6,7},{7,6},{8,9},{9,8},{10,11... | collective-permute-start | bytes 983048 | tf_op jit(solution)/shard_map/ppermute | solution.py:398
  71.4 0.0 copy-done.2
  71.4 0.9 %own.1 = (f32[8,2,62]{2,1,0:T(2,128)}, f32[264,384]{1,0:T(8,128)S(1)}) custom-call(s32[1,128]{1,0:T(1,128)S(1)} %bitcast.9, f32[640,128]{1,0:T(8,128)S(1)} %bitcast.7), custom_call_target="tpu_custom_call" | custom-call | flops 400000000 | bytes 800000 | tf_op jit(solution)/shard_map/own/pallas_call | solution.py:399
  72.3 0.3 collective-permute-done.1.other_ref
  72.6 7.1 %array.1 = f32[2,16]{1,0:T(2,128)} custom-call(f32[264,384]{1,0:T(8,128)S(1)} %get-tuple-element.5.start_ref, f32[640,128]{1,0:T(8,128)S(1)} %collective-permute-done.1.other_ref), custom_call_target="tpu_custom_call" | custom-call | tf_op jit(solution)/shard_map/array/pallas_call | solution.py:411
Async XLA Ops:
  0.6 1.0 %copy-start = (s32[32,8]{0,1:T(8,128)S(1)}, s32[32,8]{0,1:T(8,128)}, u32[]{:S(2)}) copy-start(s32[32,8]{0,1:T(8,128)} %param.5) | copy-start | bytes 3076
  33.7 5.3 %copy-start.1 = (f32[8]{0:T(128)S(1)}, f32[8]{0:T(128)}, u32[]{:S(2)}) copy-start(f32[8]{0:T(128)} %loading_ref.1) | copy-start | bytes 100
  33.9 5.1 %collective-permute-start = (f32[64,512]{1,0:T(8,128)S(1)}, f32[64,512]{1,0:T(8,128)S(1)}, u32[]{:S(2)}, u32[]{:S(2)}) collective-permute-start(f32[64,512]{1,0:T(8,128)S(1)} %beams.1.own_ref), channel_id=1, source_target_pairs={{0,1},{1,0},{2,3},{3,2},{4,5},{5,4},{6,7},{7,6},{8,9},{9,8},{10,11... | collective-permute-start | bytes 393224 | tf_op jit(solution)/shard_map/ppermute | solution.py:386
  67.5 3.9 %copy-start.2 = (s32[128]{0:T(128)S(1)}, s32[128]{0:T(128)}, u32[]{:S(2)}) copy-start(s32[128]{0:T(128)} %param.6) | copy-start | bytes 1540
  67.5 5.1 %collective-permute-start.1 = (f32[640,128]{1,0:T(8,128)S(1)}, f32[640,128]{1,0:T(8,128)S(1)}, u32[]{:S(2)}, u32[]{:S(2)}) collective-permute-start(f32[640,128]{1,0:T(8,128)S(1)} %bitcast.6), channel_id=1, source_target_pairs={{0,1},{1,0},{2,3},{3,2},{4,5},{5,4},{6,7},{7,6},{8,9},{9,8},{10,11... | collective-permute-start | bytes 983048 | tf_op jit(solution)/shard_map/ppermute | solution.py:398

commit v5 on v4

--- a/solution.py
+++ b/solution.py
@@ -21,10 +21,6 @@
 
 def vmem():
     return pl.BlockSpec(memory_space=pltpu.VMEM)
-
-
-def smem():
-    return pl.BlockSpec(memory_space=pltpu.SMEM)
 
 
 def limit(mebibytes):
@@ -140,7 +136,12 @@
     return jnp.where(((quarter + 1) & 2) == 0, value, -value)
 
 
-def message_kernel(samples_ref, codes_ref, out_ref):
+def message_kernel(samples_ref, codes_ref, panel_codes_ref, loading_ref, out_ref, side_ref):
+    side_ref[0:1, :] = cosine_of(panel_codes_ref[...])
+    side_ref[1:2, :] = cosine_of(panel_codes_ref[...] - 16)
+    own = lax.broadcasted_iota(jnp.int32, (1, 8), 1) == lax.axis_index("tile_y")
+    load = jnp.sum(jnp.where(own, loading_ref[...], 0.0), axis=1, keepdims=True)
+    side_ref[2:8, :] = jnp.broadcast_to(load, (6, 128))
     codes = jnp.concatenate([codes_ref[...], jnp.zeros((8, 96), jnp.int32)], axis=1)
     row = lax.broadcasted_iota(jnp.int32, (8, 128), 0)
     lane = lax.broadcasted_iota(jnp.int32, (8, 128), 1)
@@ -180,14 +181,14 @@
     )[:64]
 
 
-def cancel_kernel(loading_ref, own_ref, other_ref, out_ref):
-    load = loading_ref[lax.axis_index("tile_y")]
+def cancel_kernel(side_ref, beams_ref, out_ref):
+    load = side_ref[2:3, 0:64]
     core = lax.axis_index("core")
-    beams = own_ref[...] + other_ref[...]
+    beams = beams_ref[0] + beams_ref[1]
     covar = square(beams) / SNAPS
     row = lax.broadcasted_iota(jnp.int32, (64, 64), 0)
     column = lax.broadcasted_iota(jnp.int32, (64, 64), 1)
-    covar = covar + jnp.where(row == column, load, 0.0)
+    covar = covar + jnp.where(row == column, jnp.broadcast_to(load, (64, 64)), 0.0)
     covar = jnp.concatenate([covar, jnp.zeros((64, 64), jnp.float32)], axis=1)
     half = jnp.where(core == 0, beams[:, :256], beams[:, 256:])
     row = lax.broadcasted_iota(jnp.int32, (64, 128), 0)
@@ -219,54 +220,6 @@
     )
 
 
-def flat_half(ref):
-    return jnp.concatenate(
-        [
-            jnp.concatenate(
-                [ref[pl.ds(2 * b + k, 128, stride=5), :] for b in range(2)], axis=1
-            )
-            for k in range(2)
-        ],
-        axis=0,
-    )
-
-
-def own_columns(flat, half):
-    y = lax.axis_index("tile_y")
-    slot = (y % 2) * 4 + lax.axis_index("tile_z") * 2 + lax.axis_index("core")
-    mine = jnp.where((y % 4) // 2 == 0, flat[:, :128], flat[:, 128:])
-    mine = pltpu.roll(mine, lax.rem(128 - 16 * slot, 128), 1)
-    lane = lax.broadcasted_iota(jnp.int32, (256, 128), 1)
-    return jnp.where((lane < 16) & (half == y // 4), mine, 0.0)
-
-
-def own_kernel(codes_ref, own_ref, cancel_ref, out_ref):
-    cancel = own_ref[pl.ds(lax.axis_index("panel") * 40 + 4, 8, stride=5), :]
-    cancel_ref[:, 0, :] = cancel[:, :62]
-    cancel_ref[:, 1, :] = pltpu.roll(cancel, 64, 1)[:, :62]
-    own = flat_half(own_ref)
-    row = lax.broadcasted_iota(jnp.int32, (256, 256), 0)
-    column = lax.broadcasted_iota(jnp.int32, (256, 256), 1)
-    out_ref[0:256, 0:256] = square(own) / SNAPS + jnp.where(row == column, ARRAY_LOAD, 0.0)
-    cosine = cosine_of(codes_ref[...])
-    sine = cosine_of(codes_ref[...] - 16)
-    spread_cosine = jnp.broadcast_to(cosine, (128, 128)).T
-    spread_sine = jnp.broadcast_to(sine, (128, 128)).T
-    mine = own_columns(own, lax.axis_index("core"))
-    lane = lax.broadcasted_iota(jnp.int32, (128, 128), 1)
-
-    def right_side(values, first, second):
-        return jnp.where(lane == 16, first, jnp.where(lane == 17, second, values))
-
-    out_ref[0:128, 256:384] = right_side(mine[:128], spread_cosine, -spread_sine)
-    out_ref[128:256, 256:384] = right_side(mine[128:], spread_sine, spread_cosine)
-    out_ref[256:264, :] = jnp.zeros((8, 384), jnp.float32)
-    out_ref[256:257, 0:128] = cosine
-    out_ref[256:257, 128:256] = sine
-    out_ref[257:258, 0:128] = -sine
-    out_ref[257:258, 128:256] = cosine
-
-
 def split(value):
     high = value.astype(jnp.bfloat16)
     rest = value - high.astype(jnp.float32)
@@ -303,14 +256,46 @@
     )
 
 
-def array_kernel(start_ref, other_ref, out_ref, work_ref):
-    other = flat_half(other_ref)
-    work_ref[0:256, 0:256] = start_ref[0:256, 0:256] + square(other) / SNAPS
-    work_ref[0:256, 256:384] = start_ref[0:256, 256:384] + own_columns(
-        other, 1 - lax.axis_index("core")
-    )
-    work_ref[256:264, :] = start_ref[256:264, :]
-    work_ref[264:272, :] = jnp.zeros((8, 384), jnp.float32)
+def array_kernel(side_ref, lines_ref, cancel_ref, out_ref, work_ref):
+    y = lax.axis_index("tile_y")
+    cancel = lines_ref[pl.ds(lax.axis_index("panel") * 40 + 4, 8, stride=5), :]
+    cancel_ref[:, 0, :] = cancel[:, :62]
+    cancel_ref[:, 1, :] = pltpu.roll(cancel, 64, 1)[:, :62]
+
+    blocks = [
+        [lines_ref[pl.ds(640 * h + 2 * b + k, 128, stride=5), :] for h in range(2) for b in range(2)]
+        for k in range(2)
+    ]
+    flat = jnp.concatenate([jnp.concatenate(row, axis=1) for row in blocks], axis=0)
+    row = lax.broadcasted_iota(jnp.int32, (256, 256), 0)
+    column = lax.broadcasted_iota(jnp.int32, (256, 256), 1)
+    work_ref[0:256, 0:256] = square(flat) / SNAPS + jnp.where(row == column, ARRAY_LOAD, 0.0)
+
+    cosine = side_ref[0:1, :]
+    sine = side_ref[1:2, :]
+    spread_cosine = jnp.broadcast_to(cosine, (128, 128)).T
+    spread_sine = jnp.broadcast_to(sine, (128, 128)).T
+    block = y // 2
+    slot = (y % 2) * 4 + lax.axis_index("tile_z") * 2 + lax.axis_index("core")
+    mine = jnp.where(
+        block < 2,
+        jnp.where(block == 0, flat[:, 0:128], flat[:, 128:256]),
+        jnp.where(block == 2, flat[:, 256:384], flat[:, 384:512]),
+    )
+    mine = pltpu.roll(mine, lax.rem(128 - 16 * slot, 128), 1)
+    lane = lax.broadcasted_iota(jnp.int32, (128, 128), 1)
+
+    def right_side(values, first, second):
+        values = jnp.where(lane < 16, values, 0.0)
+        return jnp.where(lane == 16, first, jnp.where(lane == 17, second, values))
+
+    work_ref[0:128, 256:384] = right_side(mine[:128], spread_cosine, -spread_sine)
+    work_ref[128:256, 256:384] = right_side(mine[128:], spread_sine, spread_cosine)
+    work_ref[256:ROWS, :] = jnp.zeros((ROWS - 256, 384), jnp.float32)
+    work_ref[256:257, 0:128] = cosine
+    work_ref[256:257, 128:256] = sine
+    work_ref[257:258, 0:128] = -sine
+    work_ref[257:258, 128:256] = cosine
 
     for base in range(0, 256, CHUNK):
         stop = base + CHUNK
@@ -366,14 +351,22 @@
 
 
 def body(snapshots, beam_codes, panel_codes, loading):
-    message = pl.pallas_call(
+    message, side = pl.pallas_call(
         message_kernel,
-        out_shape=jax.ShapeDtypeStruct((16, 80, 128), jnp.bfloat16),
-        in_specs=[vmem(), vmem()],
-        out_specs=vmem(),
+        out_shape=(
+            jax.ShapeDtypeStruct((16, 80, 128), jnp.bfloat16),
+            jax.ShapeDtypeStruct((8, 128), jnp.float32),
+        ),
+        in_specs=[vmem()] * 4,
+        out_specs=(vmem(), vmem()),
         compiler_params=limit(4),
         name="message",
-    )(snapshots.reshape(8, 16, SNAPS), beam_codes.T)
+    )(
+        snapshots.reshape(8, 16, SNAPS),
+        beam_codes.T,
+        panel_codes.reshape(1, 128),
+        loading.reshape(1, 8),
+    )
     got = lax.all_to_all(message, ("tile_y", "tile_z"), 0, 0, tiled=True)
     beams = pl.pallas_call(
         beams_kernel,
@@ -383,40 +376,30 @@
         compiler_params=limit(4),
         name="beams",
     )(got)
-    other = lax.ppermute(beams, "core", [(0, 1), (1, 0)])
+    beams = lax.all_gather(beams, "core")
     lines = pl.pallas_call(
         cancel_kernel,
         out_shape=jax.ShapeDtypeStruct((640, 128), jnp.float32),
-        in_specs=[smem(), vmem(), vmem()],
+        in_specs=[vmem(), vmem()],
         out_specs=vmem(),
         compiler_params=limit(4),
         name="cancel",
-    )(loading, beams, other)
+    )(side, beams)
     lines = lines.reshape(128, 5, 1, 128)
     gathered = lax.all_to_all(lines, ("panel", "tile_y"), 0, 0, tiled=True)
-    gathered = gathered.reshape(640, 128)
-    other = lax.ppermute(gathered, "core", [(0, 1), (1, 0)])
-    cancel, start = pl.pallas_call(
-        own_kernel,
+    gathered = lax.all_gather(gathered.reshape(640, 128), "core", tiled=True)
+    cancel, beam_out = pl.pallas_call(
+        array_kernel,
         out_shape=(
             jax.ShapeDtypeStruct((8, 2, 62), jnp.float32),
-            jax.ShapeDtypeStruct((264, 384), jnp.float32),
+            jax.ShapeDtypeStruct((2, 16), jnp.float32),
         ),
         in_specs=[vmem(), vmem()],
         out_specs=(vmem(), vmem()),
-        compiler_params=limit(8),
-        cost_estimate=pl.CostEstimate(flops=400000000, bytes_accessed=800000, transcendentals=0),
-        name="own",
-    )(panel_codes.reshape(1, 128), gathered)
-    beam_out = pl.pallas_call(
-        array_kernel,
-        out_shape=jax.ShapeDtypeStruct((2, 16), jnp.float32),
-        in_specs=[vmem(), vmem()],
-        out_specs=vmem(),
         scratch_shapes=[pltpu.VMEM((ROWS, 384), jnp.float32)],
         compiler_params=limit(8),
         name="array",
-    )(start, other)
+    )(side, gathered)
     return cancel.transpose(0, 2, 1), beam_out
 
 

time: 79.9 us -> 77.6 us (0.971)
  starting transfers between devices: 7.99 us -> 0 us
  blocking collectives: 58.1 us -> 65.7 us
  waiting for transfers between devices: 1.31 us -> 0 us
  Pallas kernels: 10.6 us -> 9.38 us
    ppermute x2 -> x0, starting transfers between devices: 7.99 us -> none  [the longest x1 4.12 us: body(): other = lax.ppermute(beams, 'core', [(0, 1), (1, 0)])]
    all_gather x0 -> x2, blocking collectives: none -> 7.58 us  [the longest x1 3.84 us: body(): beams = lax.all_gather(beams, 'core')]
    ppermute x2 -> x0, waiting for transfers between devices: 1.31 us -> none  [the longest x1 0.96 us: body(): other = lax.ppermute(beams, 'core', [(0, 1), (1, 0)])]
    pallas_call x3 -> x2, Pallas kernels: 8.05 us -> 7.41 us  [the longest x1 7.31 us: body(): pl.pallas_call(array_kernel, out_shape=(jax.ShapeDtypeStruct((8, 2, 62),...]
  transfers between devices with their start and end apart: 2 -> 0, of which waited for: 2 -> 0; matrix products, arithmetic and copies ran while one was open for 0% -> 0% of each run, Pallas kernels for 1% -> 0%
where the time goes in v5:
time: 77.6 us; the launch traced here: 77.4 us
  blocking collectives  65.7 us (85%)
  Pallas kernels  9.38 us (12%)
  local copies, waits for them, and re-layouts  1.63 us (2%)
    all_to_all x1, blocking collectives, body(): got = lax.all_to_all(message, ('tile_y', 'tile_z'), 0, 0, tiled=True)  32 us
    all_to_all x1, blocking collectives, body(): gathered = lax.all_to_all(lines, ('panel', 'tile_y'), 0, 0, tiled=True)  26.2 us
    pallas_call x1, Pallas kernels, body(): pl.pallas_call(array_kernel, out_shape=(jax.ShapeDtypeStruct((8, 2, 62),...  7.31 us
    all_gather x1, blocking collectives, body(): beams = lax.all_gather(beams, 'core')  3.84 us
    all_gather x1, blocking collectives, body(): gathered = lax.all_gather(gathered.reshape(640, 128), 'core', tiled=True)  3.73 us
    pallas_call x1, Pallas kernels, body(): pl.pallas_call(cancel_kernel, out_shape=jax.ShapeDtypeStruct((640, 128),...  1.77 us

profile of v5, /device:TPU:1, one launch (start us, length us, event | category | flops | bytes accessed | tf_op | source)
XLA Modules:
  0.0 77.4 jit_solution(16197772206111830225)
XLA Ops:
  0.6 1.0 %reshape.19.samples_ref = bf16[8,16,512]{2,1,0:T(8,128)(2,1)S(1)} reshape(bf16[8,8,2,512]{3,2,1,0:T(2,128)(2,1)} %param.4) | data formatting | bytes 262144 | tf_op jit(solution)/shard_map/reshape | solution.py:365
  1.6 0.0 copy-start
  1.6 0.0 copy-start.1
  1.6 0.0 copy-start.2
  1.6 0.7 copy-done
  2.3 0.0 copy-done.1
  2.3 0.0 copy-done.2
  2.3 0.1 message.1
  2.4 32.0 %all_to_all.10.got_ref = bf16[16,80,128]{2,1,0:T(8,128)(2,1)S(1)} all-to-all(bf16[16,80,128]{2,1,0:T(8,128)(2,1)S(1)} %get-tuple-element.7), channel_id=1, replica_groups=mesh['panel'=16,'tile_y'=8,'tile_z'=2,'core'=2] {'tile_y','tile_z'}, dimensions={0} | all-to-all | bytes 655360 | tf_op jit(solution)/shard_map/all_to_all | solution.py:370
  34.4 0.2 beams.1
  34.6 3.8 %all-gather = f32[128,512]{1,0:T(8,128)S(1)} all-gather(f32[64,512]{1,0:T(8,128)S(1)} %beams.1), channel_id=2, replica_groups=mesh['panel'=16,'tile_y'=8,'tile_z'=2,'core'=2] {'core'}, dimensions={0}, use_global_device_ids=true | all-gather | bytes 393216 | tf_op jit(solution)/shard_map/all_gather | solution.py:379
  38.4 1.8 %cancel.1 = f32[640,128]{1,0:T(8,128)S(1)} custom-call(f32[8,128]{1,0:T(8,128)S(1)} %get-tuple-element.6.side_ref, f32[2,64,512]{2,1,0:T(8,128)S(1)} %bitcast.8), custom_call_target="tpu_custom_call" | custom-call | tf_op jit(solution)/shard_map/cancel/pallas_call | solution.py:380
  40.2 26.2 %all_to_all.11 = f32[128,5,1,128]{3,2,1,0:T(1,128)S(1)} all-to-all(f32[128,5,1,128]{3,2,1,0:T(1,128)S(1)} %bitcast.7), channel_id=1, replica_groups=mesh['panel'=16,'tile_y'=8,'tile_z'=2,'core'=2] {'panel','tile_y'}, dimensions={0} | all-to-all | bytes 655360 | tf_op jit(solution)/shard_map/all_to_all | solution.py:389
  66.4 3.7 %all_gather.11.lines_ref = f32[1280,128]{1,0:T(8,128)S(1)} all-gather(f32[640,128]{1,0:T(8,128)S(1)} %bitcast.12), channel_id=1, replica_groups=mesh['panel'=16,'tile_y'=8,'tile_z'=2,'core'=2] {'core'}, dimensions={0}, use_global_device_ids=true | all-gather | bytes 983040 | tf_op jit(solution)/shard_map/all_gather | solution.py:390
  70.1 7.3 %array.1 = (f32[8,2,62]{2,1,0:T(2,128)}, f32[2,16]{1,0:T(2,128)}) custom-call(f32[8,128]{1,0:T(8,128)S(1)} %get-tuple-element.6.side_ref, f32[1280,128]{1,0:T(8,128)S(1)} %all_gather.11.lines_ref), custom_call_target="tpu_custom_call" | custom-call | tf_op jit(solution)/shard_map/array/pallas_call | solution.py:391
Async XLA Ops:
  1.6 0.7 copy-start
  1.6 0.7 copy-start.1
  1.6 0.7 copy-start.2

commit v6 on v5

--- a/solution.py
+++ b/solution.py
@@ -136,7 +136,14 @@
     return jnp.where(((quarter + 1) & 2) == 0, value, -value)
 
 
-def message_kernel(samples_ref, codes_ref, panel_codes_ref, loading_ref, out_ref, side_ref):
+def identity_kernel(out_ref):
+    row = lax.broadcasted_iota(jnp.int32, (64, 128), 0)
+    column = lax.broadcasted_iota(jnp.int32, (64, 128), 1) & 63
+    source = jnp.where(column < 62, column // 2 + 31 * (column & 1), 64)
+    out_ref[...] = jnp.where(row == source, 1.0, 0.0)
+
+
+def message_kernel(_, samples_ref, codes_ref, panel_codes_ref, loading_ref, out_ref, side_ref):
     side_ref[0:1, :] = cosine_of(panel_codes_ref[...])
     side_ref[1:2, :] = cosine_of(panel_codes_ref[...] - 16)
     own = lax.broadcasted_iota(jnp.int32, (1, 8), 1) == lax.axis_index("tile_y")
@@ -162,11 +169,10 @@
     table = jnp.concatenate([columns(0), columns(4)], axis=0)
     table = (table / math.sqrt(256)).astype(jnp.bfloat16)
     for p in range(8):
+        samples = samples_ref[p].reshape(16, SNAPS)
         for z in range(2):
             for b in range(4):
-                out_ref[2 * p + z, 16 * b : 16 * b + 16, :] = samples_ref[
-                    p, :, 128 * b : 128 * b + 128
-                ]
+                out_ref[2 * p + z, 16 * b : 16 * b + 16, :] = samples[:, 128 * b : 128 * b + 128]
             out_ref[2 * p + z, 64:80, :] = table
 
 
@@ -181,7 +187,7 @@
     )[:64]
 
 
-def cancel_kernel(side_ref, beams_ref, out_ref):
+def cancel_kernel(side_ref, identity_ref, beams_ref, out_ref):
     load = side_ref[2:3, 0:64]
     core = lax.axis_index("core")
     beams = beams_ref[0] + beams_ref[1]
@@ -191,11 +197,7 @@
     covar = covar + jnp.where(row == column, jnp.broadcast_to(load, (64, 64)), 0.0)
     covar = jnp.concatenate([covar, jnp.zeros((64, 64), jnp.float32)], axis=1)
     half = jnp.where(core == 0, beams[:, :256], beams[:, 256:])
-    row = lax.broadcasted_iota(jnp.int32, (64, 128), 0)
-    column = lax.broadcasted_iota(jnp.int32, (64, 128), 1) & 63
-    source = jnp.where(column < 62, column // 2 + 31 * (column & 1), 64)
-    identity = jnp.where(row == source, 1.0, 0.0)
-    whole = jnp.concatenate([covar, half, identity], axis=1)
+    whole = jnp.concatenate([covar, half, identity_ref[...]], axis=1)
     rows = [
         [whole[8 * i : 8 * i + 8, 128 * g : 128 * g + 128] for g in range(4)] for i in range(8)
     ]
@@ -351,18 +353,29 @@
 
 
 def body(snapshots, beam_codes, panel_codes, loading):
+    identity = pl.pallas_call(
+        identity_kernel,
+        out_shape=jax.ShapeDtypeStruct((64, 128), jnp.float32),
+        out_specs=vmem(),
+        compiler_params=limit(4),
+        cost_estimate=pl.CostEstimate(
+            flops=2000000000, bytes_accessed=4000000, transcendentals=0
+        ),
+        name="identity",
+    )()
     message, side = pl.pallas_call(
         message_kernel,
         out_shape=(
             jax.ShapeDtypeStruct((16, 80, 128), jnp.bfloat16),
             jax.ShapeDtypeStruct((8, 128), jnp.float32),
         ),
-        in_specs=[vmem()] * 4,
+        in_specs=[vmem()] * 5,
         out_specs=(vmem(), vmem()),
         compiler_params=limit(4),
         name="message",
     )(
-        snapshots.reshape(8, 16, SNAPS),
+        identity,
+        snapshots,
         beam_codes.T,
         panel_codes.reshape(1, 128),
         loading.reshape(1, 8),
@@ -380,11 +393,11 @@
     lines = pl.pallas_call(
         cancel_kernel,
         out_shape=jax.ShapeDtypeStruct((640, 128), jnp.float32),
-        in_specs=[vmem(), vmem()],
+        in_specs=[vmem(), vmem(), vmem()],
         out_specs=vmem(),
         compiler_params=limit(4),
         name="cancel",
-    )(side, beams)
+    )(side, identity, beams)
     lines = lines.reshape(128, 5, 1, 128)
     gathered = lax.all_to_all(lines, ("panel", "tile_y"), 0, 0, tiled=True)
     gathered = lax.all_gather(gathered.reshape(640, 128), "core", tiled=True)

time: 77.6 us -> 76.9 us (level)
    reshape x1 -> x0, local copies, waits for them, and re-layouts: 0.96 us -> none  [body(): snapshots.reshape(8, 16, SNAPS)]
where the time goes in v6:
time: 76.9 us; the launch traced here: 76.7 us
  blocking collectives  65.7 us (85%)
  Pallas kernels  9.41 us (12%)
  local copies, waits for them, and re-layouts  0.86 us (1%)
    all_to_all x1, blocking collectives, body(): got = lax.all_to_all(message, ('tile_y', 'tile_z'), 0, 0, tiled=True)  32 us
    all_to_all x1, blocking collectives, body(): gathered = lax.all_to_all(lines, ('panel', 'tile_y'), 0, 0, tiled=True)  26.2 us
    pallas_call x1, Pallas kernels, body(): pl.pallas_call(array_kernel, out_shape=(jax.ShapeDtypeStruct((8, 2, 62),...  7.31 us
    all_gather x1, blocking collectives, body(): beams = lax.all_gather(beams, 'core')  3.84 us
    all_gather x1, blocking collectives, body(): gathered = lax.all_gather(gathered.reshape(640, 128), 'core', tiled=True)  3.73 us
    pallas_call x1, Pallas kernels, body(): pl.pallas_call(cancel_kernel, out_shape=jax.ShapeDtypeStruct((640, 128),...  1.77 us

profile of v6, /device:TPU:1, one launch (start us, length us, event | category | flops | bytes accessed | tf_op | source)
XLA Modules:
  0.0 76.7 jit_solution(8412560532353194924)
XLA Ops:
  0.6 0.0 copy-start
  0.7 0.0 copy-start.1
  0.7 0.0 copy-start.2
  0.7 0.0 copy-start.3
  0.7 0.8 %copy-done = bf16[8,8,2,512]{3,2,1,0:T(2,128)(2,1)S(1)} copy-done((bf16[8,8,2,512]{3,2,1,0:T(2,128)(2,1)S(1)}, bf16[8,8,2,512]{3,2,1,0:T(2,128)(2,1)}, u32[]{:S(2)}) %copy-start) | copy-done | bytes 131096
  1.5 0.0 copy-done.1
  1.5 0.0 copy-done.2
  1.5 0.0 copy-done.3
  1.5 0.1 message.1
  1.7 32.0 %all_to_all.10.got_ref = bf16[16,80,128]{2,1,0:T(8,128)(2,1)S(1)} all-to-all(bf16[16,80,128]{2,1,0:T(8,128)(2,1)S(1)} %get-tuple-element.7), channel_id=1, replica_groups=mesh['panel'=16,'tile_y'=8,'tile_z'=2,'core'=2] {'tile_y','tile_z'}, dimensions={0} | all-to-all | bytes 655360 | tf_op jit(solution)/shard_map/all_to_all | solution.py:383
  33.6 0.2 beams.1
  33.9 3.8 %all-gather = f32[128,512]{1,0:T(8,128)S(1)} all-gather(f32[64,512]{1,0:T(8,128)S(1)} %beams.1), channel_id=2, replica_groups=mesh['panel'=16,'tile_y'=8,'tile_z'=2,'core'=2] {'core'}, dimensions={0}, use_global_device_ids=true | all-gather | bytes 393216 | tf_op jit(solution)/shard_map/all_gather | solution.py:392
  37.7 1.8 %cancel.1 = f32[640,128]{1,0:T(8,128)S(1)} custom-call(f32[8,128]{1,0:T(8,128)S(1)} %get-tuple-element.6.side_ref, f32[64,128]{1,0:T(8,128)S(1)} %identity.1._.identity_ref, f32[2,64,512]{2,1,0:T(8,128)S(1)} %bitcast.8), custom_call_target="tpu_custom_call" | custom-call | tf_op jit(solution)/shard_map/cancel/pallas_call | solution.py:393
  39.5 26.2 %all_to_all.11 = f32[128,5,1,128]{3,2,1,0:T(1,128)S(1)} all-to-all(f32[128,5,1,128]{3,2,1,0:T(1,128)S(1)} %bitcast.7), channel_id=1, replica_groups=mesh['panel'=16,'tile_y'=8,'tile_z'=2,'core'=2] {'panel','tile_y'}, dimensions={0} | all-to-all | bytes 655360 | tf_op jit(solution)/shard_map/all_to_all | solution.py:402
  65.6 3.7 %all_gather.11.lines_ref = f32[1280,128]{1,0:T(8,128)S(1)} all-gather(f32[640,128]{1,0:T(8,128)S(1)} %bitcast.12), channel_id=1, replica_groups=mesh['panel'=16,'tile_y'=8,'tile_z'=2,'core'=2] {'core'}, dimensions={0}, use_global_device_ids=true | all-gather | bytes 983040 | tf_op jit(solution)/shard_map/all_gather | solution.py:403
  69.4 7.3 %array.1 = (f32[8,2,62]{2,1,0:T(2,128)}, f32[2,16]{1,0:T(2,128)}) custom-call(f32[8,128]{1,0:T(8,128)S(1)} %get-tuple-element.6.side_ref, f32[1280,128]{1,0:T(8,128)S(1)} %all_gather.11.lines_ref), custom_call_target="tpu_custom_call" | custom-call | tf_op jit(solution)/shard_map/array/pallas_call | solution.py:404
  (1 shorter events, 0.0 us)
Async XLA Ops:
  0.6 0.9 %copy-start = (bf16[8,8,2,512]{3,2,1,0:T(2,128)(2,1)S(1)}, bf16[8,8,2,512]{3,2,1,0:T(2,128)(2,1)}, u32[]{:S(2)}) copy-start(bf16[8,8,2,512]{3,2,1,0:T(2,128)(2,1)} %samples_ref.1) | copy-start | bytes 393220
  0.7 0.9 %copy-start.1 = (s32[32,8]{0,1:T(8,128)S(1)}, s32[32,8]{0,1:T(8,128)}, u32[]{:S(2)}) copy-start(s32[32,8]{0,1:T(8,128)} %param.5) | copy-start | bytes 3076
  0.7 0.9 %copy-start.2 = (s32[128]{0:T(128)S(1)}, s32[128]{0:T(128)}, u32[]{:S(2)}) copy-start(s32[128]{0:T(128)} %param.6) | copy-start | bytes 1540
  0.7 0.9 %copy-start.3 = (f32[8]{0:T(128)S(1)}, f32[8]{0:T(128)}, u32[]{:S(2)}) copy-start(f32[8]{0:T(128)} %param.7) | copy-start | bytes 100

commit v7 on v6

--- a/solution.py
+++ b/solution.py
@@ -99,10 +99,9 @@
 
 
 def less_product(value, spread, lines):
-    terms = [f * line for f, line in zip(spread, lines)]
-    while len(terms) > 1:
-        terms = [sum(terms[i : i + 2]) for i in range(0, len(terms), 2)]
-    return value - terms[0]
+    for f, line in zip(spread, lines):
+        value = value - f * line
+    return value
 
 
 def forward(rows, steps):

time: 76.9 us -> 76.9 us (level)
  no operation moved by 1% of the time
where the time goes in v7:
time: 76.9 us; the launch traced here: 76.7 us
  blocking collectives  65.7 us (85%)
  Pallas kernels  9.44 us (12%)
  local copies, waits for them, and re-layouts  0.86 us (1%)
    all_to_all x1, blocking collectives, body(): got = lax.all_to_all(message, ('tile_y', 'tile_z'), 0, 0, tiled=True)  32 us
    all_to_all x1, blocking collectives, body(): gathered = lax.all_to_all(lines, ('panel', 'tile_y'), 0, 0, tiled=True)  26.2 us
    pallas_call x1, Pallas kernels, body(): pl.pallas_call(array_kernel, out_shape=(jax.ShapeDtypeStruct((8, 2, 62),...  7.36 us
    all_gather x1, blocking collectives, body(): beams = lax.all_gather(beams, 'core')  3.84 us
    all_gather x1, blocking collectives, body(): gathered = lax.all_gather(gathered.reshape(640, 128), 'core', tiled=True)  3.73 us
    pallas_call x1, Pallas kernels, body(): pl.pallas_call(cancel_kernel, out_shape=jax.ShapeDtypeStruct((640, 128),...  1.75 us

profile of v7, /device:TPU:1, one launch (start us, length us, event | category | flops | bytes accessed | tf_op | source)
XLA Modules:
  0.0 76.7 jit_solution(3318019769115983174)
XLA Ops:
  0.6 0.0 copy-start
  0.7 0.0 copy-start.1
  0.7 0.0 copy-start.2
  0.7 0.0 copy-start.3
  0.7 0.8 %copy-done = bf16[8,8,2,512]{3,2,1,0:T(2,128)(2,1)S(1)} copy-done((bf16[8,8,2,512]{3,2,1,0:T(2,128)(2,1)S(1)}, bf16[8,8,2,512]{3,2,1,0:T(2,128)(2,1)}, u32[]{:S(2)}) %copy-start) | copy-done | bytes 131096
  1.5 0.0 copy-done.1
  1.5 0.0 copy-done.2
  1.5 0.0 copy-done.3
  1.5 0.1 message.1
  1.7 32.0 %all_to_all.10.got_ref = bf16[16,80,128]{2,1,0:T(8,128)(2,1)S(1)} all-to-all(bf16[16,80,128]{2,1,0:T(8,128)(2,1)S(1)} %get-tuple-element.7), channel_id=1, replica_groups=mesh['panel'=16,'tile_y'=8,'tile_z'=2,'core'=2] {'tile_y','tile_z'}, dimensions={0} | all-to-all | bytes 655360 | tf_op jit(solution)/shard_map/all_to_all | solution.py:382
  33.6 0.2 beams.1
  33.9 3.8 %all-gather = f32[128,512]{1,0:T(8,128)S(1)} all-gather(f32[64,512]{1,0:T(8,128)S(1)} %beams.1), channel_id=2, replica_groups=mesh['panel'=16,'tile_y'=8,'tile_z'=2,'core'=2] {'core'}, dimensions={0}, use_global_device_ids=true | all-gather | bytes 393216 | tf_op jit(solution)/shard_map/all_gather | solution.py:391
  37.7 1.8 %cancel.1 = f32[640,128]{1,0:T(8,128)S(1)} custom-call(f32[8,128]{1,0:T(8,128)S(1)} %get-tuple-element.6.side_ref, f32[64,128]{1,0:T(8,128)S(1)} %identity.1._.identity_ref, f32[2,64,512]{2,1,0:T(8,128)S(1)} %bitcast.8), custom_call_target="tpu_custom_call" | custom-call | tf_op jit(solution)/shard_map/cancel/pallas_call | solution.py:392
  39.5 26.2 %all_to_all.11 = f32[128,5,1,128]{3,2,1,0:T(1,128)S(1)} all-to-all(f32[128,5,1,128]{3,2,1,0:T(1,128)S(1)} %bitcast.7), channel_id=1, replica_groups=mesh['panel'=16,'tile_y'=8,'tile_z'=2,'core'=2] {'panel','tile_y'}, dimensions={0} | all-to-all | bytes 655360 | tf_op jit(solution)/shard_map/all_to_all | solution.py:401
  65.6 3.7 %all_gather.11.lines_ref = f32[1280,128]{1,0:T(8,128)S(1)} all-gather(f32[640,128]{1,0:T(8,128)S(1)} %bitcast.12), channel_id=1, replica_groups=mesh['panel'=16,'tile_y'=8,'tile_z'=2,'core'=2] {'core'}, dimensions={0}, use_global_device_ids=true | all-gather | bytes 983040 | tf_op jit(solution)/shard_map/all_gather | solution.py:402
  69.4 7.4 %array.1 = (f32[8,2,62]{2,1,0:T(2,128)}, f32[2,16]{1,0:T(2,128)}) custom-call(f32[8,128]{1,0:T(8,128)S(1)} %get-tuple-element.6.side_ref, f32[1280,128]{1,0:T(8,128)S(1)} %all_gather.11.lines_ref), custom_call_target="tpu_custom_call" | custom-call | tf_op jit(solution)/shard_map/array/pallas_call | solution.py:403
  (1 shorter events, 0.0 us)
Async XLA Ops:
  0.6 0.9 %copy-start = (bf16[8,8,2,512]{3,2,1,0:T(2,128)(2,1)S(1)}, bf16[8,8,2,512]{3,2,1,0:T(2,128)(2,1)}, u32[]{:S(2)}) copy-start(bf16[8,8,2,512]{3,2,1,0:T(2,128)(2,1)} %samples_ref.1) | copy-start | bytes 393220
  0.7 0.9 %copy-start.1 = (s32[32,8]{0,1:T(8,128)S(1)}, s32[32,8]{0,1:T(8,128)}, u32[]{:S(2)}) copy-start(s32[32,8]{0,1:T(8,128)} %param.5) | copy-start | bytes 3076
  0.7 0.9 %copy-start.2 = (s32[128]{0:T(128)S(1)}, s32[128]{0:T(128)}, u32[]{:S(2)}) copy-start(s32[128]{0:T(128)} %param.6) | copy-start | bytes 1540
  0.7 0.9 %copy-start.3 = (f32[8]{0:T(128)S(1)}, f32[8]{0:T(128)}, u32[]{:S(2)}) copy-start(f32[8]{0:T(128)} %param.7) | copy-start | bytes 100
